TPU v7x, 256 devices: a whole 4x4x8 slice. The times are simulated.
256 devices in a mesh: dp: 32 (over y, z_hi, core), tensor: 8 (over x, z_lo).
Axes of the slice: x: 4, y: 4, z: 8 (z_hi: 4, z_lo: 2; z = z_hi * 2 + z_lo), core: 2. Of those that a mesh axis runs over, the one named last changes fastest.
Arguments:
- prefix_kv: bfloat16 [65536, 2048], P('dp', 'tensor'), may hold values from -24 to 24
- page_key_values: bfloat16 [1024, 256, 2048], P('dp', None, 'tensor'), may hold values from -6 to 6
- context_len: int32 [1024], P('dp'), may hold values from 1 to 256
- prefill_owner: int32 [1], replicated, may hold values from 0 to 31
- assign: int32 [1024, 1], P('dp'), may hold values from 0 to 31, as said below
- x_new: bfloat16 [1024, 4, 8192], P('dp', None, 'tensor'), may hold values from -6 to 6
- norm_gain: float32 [8192], replicated, may hold values from 0.1 to 1.9
- key_weight: bfloat16 [8192, 1024], P(None, 'tensor'), may hold values from -0.25 to 0.25
- value_weight: bfloat16 [8192, 1024], P(None, 'tensor'), may hold values from -0.0625 to 0.0625
- decoded_queries: bfloat16 [1024, 4, 8192], P('dp', None, 'tensor'), may hold values from -30 to 30
Outputs:
- decoded: bfloat16 [2048, 4, 8192], P('dp', None, 'tensor')
Inputs may be any that keep to these rules, and one draw needn't show every extreme that they name: `assign`: within the 32 requests of one device no group is named more than 2 times; one group, the same for every device, is named exactly 2 times by the requests of every device.
All inputs are finite; a program needn't handle non-finite values.
Results may differ from a plain program's by a relative error of at most 0.0088.
Values may be sent and summed in bfloat16 or wider, within the bound.
No kernel may reach another device: no remote copies, remote signals or barrier semaphores. Data moves between devices by JAX's collectives and lax.ppermute only.
A program may use at most 128 MiB of HBM per device.

v0:
```python
import math

import jax
import jax.numpy as jnp
from jax import lax
from jax.sharding import PartitionSpec as P

HEAD_SIZE = 128
CAP = 2


epsilon = 1e-05


def broadcast(block, axis, holder):
    block = jnp.where(lax.axis_index(axis) == holder, block, jnp.zeros_like(block))
    return lax.psum(block, axis)


def attend(queries, page_rows, recent_key_values, request_lengths, prefix):
    members = queries.shape[0]
    step_count = queries.shape[1]
    key_heads = prefix.shape[1] // (2 * HEAD_SIZE)
    group_size = queries.shape[2] // (key_heads * HEAD_SIZE)
    page_span = page_rows.shape[1]
    grouped = queries.reshape(members, step_count, key_heads, group_size, HEAD_SIZE)
    shared = prefix.reshape(prefix.shape[0], key_heads, 2, HEAD_SIZE)
    paged = page_rows.reshape(members, page_span, key_heads, 2, HEAD_SIZE)
    recent = recent_key_values.reshape(members, step_count, key_heads, 2, HEAD_SIZE)
    scaling = 1.0 / math.sqrt(HEAD_SIZE)
    shared_scores = (
        jnp.einsum("ntjgd,ljd->ntjgl", grouped, shared[:, :, 0], preferred_element_type=jnp.float32)
        * scaling
    )
    paged_scores = (
        jnp.einsum(
            "ntjgd,npjd->ntjgp", grouped, paged[:, :, :, 0], preferred_element_type=jnp.float32
        )
        * scaling
    )
    recent_scores = (
        jnp.einsum(
            "ntjgd,nsjd->ntjgs", grouped, recent[:, :, :, 0], preferred_element_type=jnp.float32
        )
        * scaling
    )
    position = jnp.arange(page_span).astype(jnp.float32)
    visible = position[None, :] < request_lengths[:, None]
    paged_scores = jnp.where(visible[:, None, None, None, :], paged_scores, -jnp.inf)
    causal = jnp.arange(step_count)[None, :] <= jnp.arange(step_count)[:, None]
    recent_scores = jnp.where(causal[None, :, None, None, :], recent_scores, -jnp.inf)
    highest = jnp.maximum(
        jnp.maximum(
            jnp.max(shared_scores, axis=-1, keepdims=True),
            jnp.max(paged_scores, axis=-1, keepdims=True),
        ),
        jnp.max(recent_scores, axis=-1, keepdims=True),
    )
    shared_exp = jnp.exp(shared_scores - highest)
    paged_exp = jnp.exp(paged_scores - highest)
    recent_exp = jnp.exp(recent_scores - highest)
    denominator = (
        jnp.sum(shared_exp, axis=-1, keepdims=True)
        + jnp.sum(paged_exp, axis=-1, keepdims=True)
        + jnp.sum(recent_exp, axis=-1, keepdims=True)
    )
    shared_weights = (shared_exp / denominator).astype(jnp.bfloat16)
    paged_weights = (paged_exp / denominator).astype(jnp.bfloat16)
    recent_weights = (recent_exp / denominator).astype(jnp.bfloat16)
    result = jnp.einsum(
        "ntjgl,ljd->ntjgd", shared_weights, shared[:, :, 1], preferred_element_type=jnp.float32
    )
    result = result + jnp.einsum(
        "ntjgp,npjd->ntjgd", paged_weights, paged[:, :, :, 1], preferred_element_type=jnp.float32
    )
    result = result + jnp.einsum(
        "ntjgs,nsjd->ntjgd", recent_weights, recent[:, :, :, 1], preferred_element_type=jnp.float32
    )
    return result.reshape(members, step_count, key_heads * group_size * HEAD_SIZE).astype(
        jnp.bfloat16
    )


def per_device(
    prefix_kv,
    page_key_values,
    context_len,
    prefill_owner,
    assign,
    x_new,
    norm_gain,
    key_weight,
    value_weight,
    decoded_queries,
):
    row_count = decoded_queries.shape[0]
    step_count = decoded_queries.shape[1]
    features = lax.all_gather(x_new, "tensor", axis=2, tiled=True).astype(jnp.float32)
    normed = (
        features
        * lax.rsqrt(jnp.mean(features * features, axis=2, keepdims=True) + epsilon)
        * norm_gain
    ).astype(jnp.bfloat16)
    flattened = normed.reshape(row_count * step_count, features.shape[2])
    fresh_keys = jnp.dot(flattened, key_weight, preferred_element_type=jnp.float32).astype(
        jnp.bfloat16
    )
    fresh_values = jnp.dot(flattened, value_weight, preferred_element_type=jnp.float32).astype(
        jnp.bfloat16
    )
    key_heads = key_weight.shape[1] // HEAD_SIZE
    recent_key_values = jnp.stack(
        [
            fresh_keys.reshape(row_count, step_count, key_heads, HEAD_SIZE),
            fresh_values.reshape(row_count, step_count, key_heads, HEAD_SIZE),
        ],
        axis=3,
    ).reshape(row_count, step_count, 2 * key_heads * HEAD_SIZE)
    prefix = broadcast(prefix_kv, "dp", prefill_owner[0])
    group_count = lax.axis_size("dp")
    assigned = assign[:, 0]
    indices = jnp.arange(row_count)
    matching = (assigned[:, None] == assigned[None, :]) & (indices[None, :] < indices[:, None])
    ranking = jnp.sum(matching.astype(jnp.int32), axis=1)
    destination = assigned * CAP + ranking
    selector = (jnp.arange(group_count * CAP)[:, None] == destination[None, :]).astype(jnp.bfloat16)

    def to_slots(payload):
        arranged = jnp.dot(
            selector, payload.reshape(row_count, -1), preferred_element_type=jnp.bfloat16
        )
        return arranged.reshape((group_count, CAP) + payload.shape[1:])

    request_lengths = context_len.astype(jnp.bfloat16)[:, None]
    page_rows = lax.all_to_all(
        to_slots(page_key_values), "dp", split_axis=0, concat_axis=0, tiled=True
    )
    queries = lax.all_to_all(
        to_slots(decoded_queries), "dp", split_axis=0, concat_axis=0, tiled=True
    )
    recent_in = lax.all_to_all(
        to_slots(recent_key_values), "dp", split_axis=0, concat_axis=0, tiled=True
    )
    lengths_in = lax.all_to_all(
        to_slots(request_lengths), "dp", split_axis=0, concat_axis=0, tiled=True
    )
    members = page_rows.shape[0] * page_rows.shape[1]
    sizes_flat = lengths_in.reshape(members)
    result = attend(
        queries.reshape((members,) + queries.shape[2:]),
        page_rows.reshape((members,) + page_rows.shape[2:]),
        recent_in.reshape((members,) + recent_in.shape[2:]),
        sizes_flat.astype(jnp.float32),
        prefix,
    )
    result = result * (sizes_flat > 0).astype(jnp.bfloat16)[:, None, None]
    decoded = result.reshape(page_rows.shape[0], page_rows.shape[1], step_count, result.shape[2])
    return decoded.reshape(group_count * CAP, step_count, decoded.shape[3])


def solution(mesh):
    in_specs = (
        P("dp", "tensor"),
        P("dp", None, "tensor"),
        P("dp"),
        P(),
        P("dp", None),
        P("dp", None, "tensor"),
        P(),
        P(None, "tensor"),
        P(None, "tensor"),
        P("dp", None, "tensor"),
    )
    out_specs = P("dp", None, "tensor")
    return jax.shard_map(
        per_device, mesh=mesh, in_specs=in_specs, out_specs=out_specs, check_vma=False
    )
```

profile of v0, /device:TPU:1, one launch (start us, length us, event | category | flops | bytes accessed | tf_op | source)
XLA Modules:
  0.0 599.3 jit_solution(11787306108835227851)
XLA Ops:
  7.4 0.7 all-gather.2.cloned.1.call-update
  8.1 0.9 convert_reduce_fusion.1
  9.0 0.7 multiply_add_fusion.1
  9.7 0.8 fusion.43
  10.5 0.1 copy.190
  10.6 0.7 copy.162
  11.3 12.8 %all-to-all-start.1 = ((bf16[32,2,1]{1,2,0:T(2,128)(2,1)}), bf16[32,2,1]{1,2,0:T(2,128)(2,1)S(1)}, u32[]{:S(2)}, u32[]{:S(2)}) async-start(bf16[32,2,1]{1,2,0:T(2,128)(2,1)} %copy.162), calls=%async_computation.1 | async-start | bytes 32768 | tf_op jit(solution)/shard_map/all_to_all | solution.py:144
  24.1 1.3 fusion.36
  25.4 1.2 copy.160
  26.6 41.9 %all-gather.2.cloned.1.call-done = bf16[32,4,8192]{2,1,0:T(4,128)(2,1)} async-done(((bf16[32,4,1024]{2,1,0:T(4,128)(2,1)}), bf16[32,4,8192]{2,1,0:T(4,128)(2,1)}) %all-gather.2.cloned.1.call-update) | async-done | bytes 2097168 | tf_op jit(solution)/shard_map/all_gather | solution.py:98
  68.5 2.8 fusion.5
  71.3 9.4 %all-to-all-start = ((bf16[32,2,4,1024]{3,2,1,0:T(4,128)(2,1)}), bf16[32,2,4,1024]{3,2,1,0:T(4,128)(2,1)S(1)}, u32[]{:S(2)}, u32[]{:S(2)}) async-start(bf16[32,2,4,1024]{3,2,1,0:T(4,128)(2,1)} %copy.160), calls=%async_computation | async-start | bytes 1048576 | tf_op jit(solution)/shard_map/all_to_all | solution.py:138
  80.8 4.4 fusion.7
  85.1 4.0 reshape.270
  89.1 2.4 convolution_convert_fusion
  91.5 0.1 copy.171
  91.6 0.3 copy-done.4
  91.9 0.7 convolution_convert_fusion.1
  92.6 0.1 copy.170
  92.7 0.2 pad_maximum_fusion
  92.9 0.2 fusion.41
  93.1 0.8 copy.173
  93.9 5.0 all-to-all-done
  98.8 5.1 all-to-all-start.3
  104.0 8.3 %fusion.8 = bf16[32,2,256,256]{3,0,2,1:T(8,128)(2,1)} fusion(s32[32]{0:T(128)S(1)} %multiply_add_fusion.1, s32[32,2]{0,1:T(2,128)S(1)} %multiply_add_fusion, bf16[4,8,256,256]{3,2,1,0:T(8,128)(2,1)} %bitcast.209), kind=kOutput, calls=%fused_computation.14 | convolution fusion | flops 268437504 | bytes 12583296 | tf_op jit(solution)/shard_map/dot_general | solution.py:129
  112.3 11.4 %copy.164 = bf16[32,2,256,256]{3,2,1,0:T(8,128)(2,1)} copy(bf16[32,2,256,256]{3,0,2,1:T(8,128)(2,1)} %fusion.8) | data formatting | bytes 16777216 | tf_op jit(solution)/shard_map/dot_general | solution.py:129
  123.7 0.0 all-to-all-done.3
  123.7 10.0 %all-to-all-start.2 = ((bf16[32,2,256,256]{3,2,1,0:T(8,128)(2,1)}), bf16[32,2,256,256]{3,2,1,0:T(8,128)(2,1)}, u32[]{:S(2)}, u32[]{:S(2)}) async-start(bf16[32,2,256,256]{3,2,1,0:T(8,128)(2,1)} %copy.164), calls=%async_computation.2 | async-start | bytes 16777216 | tf_op jit(solution)/shard_map/all_to_all | solution.py:135
  133.6 0.3 all-reduce.2.cloned.1.call-start
  134.6 0.6 copy.157
  135.2 0.1 broadcast_select_fusion
  135.3 1.3 copy.158
  136.6 0.0 all-reduce.2.cloned.1.call-update
  136.7 0.1 fusion.45
  136.8 0.1 reshape.278
  136.9 0.1 convert_reduce_fusion
  136.9 0.1 reshape.277
  137.0 0.1 broadcast_compare_fusion
  137.1 0.2 reshape.267
  137.3 402.4 %all-reduce.2.cloned.1.call-done = bf16[2048,1,2,128]{3,0,2,1:T(8,128)(2,1)} async-done(((bf16[2048,1,2,128]{3,0,2,1:T(8,128)(2,1)}), bf16[2048,1,2,128]{3,0,2,1:T(8,128)(2,1)}) %all-reduce.2.cloned.1.call-update) | async-done | bytes 1048592 | tf_op jit(solution)/shard_map/psum | solution.py:17
  539.7 9.1 %bitcast_reduce_fusion = (f32[64,4,8]{0,2,1:T(8,128)S(1)}, f32[2048,64,4,8]{0,1,3,2:T(8,128)}) fusion(bf16[64,4,8,128]{3,2,1,0:T(8,128)(2,1)S(1)} %reshape.267, bf16[2048,1,2,128]{3,0,2,1:T(8,128)(2,1)} %all-reduce.2.cloned.1.call-done), kind=kOutput, calls=%fused_computation.1 | convolution fusion | flops 1082128384 | bytes 17833984 | tf_op jit(solution)/shard_map/ntjgd,ljd->ntjgl/dot_general | solution.py:32
  548.8 0.1 reshape_reshape.12
  548.9 0.2 fusion.60
  549.0 2.4 fusion.61
  551.5 0.1 copy.175
  551.6 0.0 all-to-all-done.2
  551.6 11.9 %copy.165 = bf16[32,2,256,256]{2,3,1,0:T(8,128)(2,1)} copy(bf16[32,2,256,256]{3,2,1,0:T(8,128)(2,1)} %all-to-all-done.2) | data formatting | bytes 16777216 | tf_op jit(solution)/shard_map/all_to_all | solution.py:135
  563.5 4.3 bitcast_reduce_fusion.1
  567.8 0.1 copy.167
  567.9 0.1 copy.176
  568.0 7.7 %fusion.1 = f32[64,4,8]{0,2,1:T(8,128)S(1)} fusion(f32[2048,64,4,8]{0,1,3,2:T(8,128)} %get-tuple-element.10, f32[64,4,8]{0,2,1:T(8,128)S(1)} %maximum_maximum_fusion), kind=kLoop, calls=%fused_computation.4 | loop fusion | flops 12580864 | bytes 16793600 | tf_op jit(solution)/shard_map/reduce_sum | solution.py:63
  575.8 0.5 fusion.35
  576.2 0.1 copy.179
  576.3 1.0 fusion.13
  577.4 0.1 copy.177
  577.4 0.1 copy.181
  577.6 3.3 fusion.10
  580.9 0.5 fusion.38
  581.4 0.0 copy-start.1
  581.4 8.5 %fusion.23 = bf16[64,4,1,8,128]{4,0,3,1,2:T(8,128)(2,1)S(1)} fusion(f32[64,4,8]{0,2,1:T(8,128)S(1)} %add_add_fusion, f32[64,4,8]{0,2,1:T(8,128)S(1)} %maximum_maximum_fusion, f32[2048,64,4,8]{0,1,3,2:T(8,128)} %get-tuple-element.10, f32[64,128,4,8]{1,3,2,0:T(8,128)S(1)} %fusion.38, f32[64,128,4,8]{1,3,2,0:T(8,128)S(1)} %fusion.10, ...), kind=kOutput, calls=%fused_computation.29 | convolution fusion | flops 1091305472 | bytes 19955712 | tf_op jit(solution)/shard_map/ntjgl,ljd->ntjgd/dot_general | solution.py:70
  590.0 0.3 copy.186
  590.3 0.2 convert_element_type.74
  590.5 0.1 broadcast_multiply_fusion
  590.7 1.2 copy.187
  (23 shorter events, 0.1 us)
Async XLA Ops:
  7.4 81.7 %copy-start = (bf16[8192,128]{1,0:T(8,128)(2,1)S(1)}, bf16[8192,128]{1,0:T(8,128)(2,1)}, u32[]{:S(2)}) copy-start(bf16[8192,128]{1,0:T(8,128)(2,1)} %param.18) | copy-start | bytes 6291460
  7.4 73.4 %copy-start.7 = (f32[8192]{0:T(1024)S(1)}, f32[8192]{0:T(1024)}, u32[]{:S(2)}) copy-start(f32[8192]{0:T(1024)} %param.16) | copy-start | bytes 98308
  7.4 61.1 %all-gather.2.cloned.1.call-start = ((), (), s32[]{:S(2)}) async-start(), calls=%async_computation.5 | async-start | bytes 2359296 | tf_op jit(solution)/shard_map/all_gather | solution.py:98
  11.3 59.9 %all-to-all-start.1 = ((bf16[32,2,1]{1,2,0:T(2,128)(2,1)}), bf16[32,2,1]{1,2,0:T(2,128)(2,1)S(1)}, u32[]{:S(2)}, u32[]{:S(2)}) async-start(bf16[32,2,1]{1,2,0:T(2,128)(2,1)} %copy.162), calls=%async_computation.1 | async-start | bytes 32768 | tf_op jit(solution)/shard_map/all_to_all | solution.py:144
  71.3 27.6 %all-to-all-start = ((bf16[32,2,4,1024]{3,2,1,0:T(4,128)(2,1)}), bf16[32,2,4,1024]{3,2,1,0:T(4,128)(2,1)S(1)}, u32[]{:S(2)}, u32[]{:S(2)}) async-start(bf16[32,2,4,1024]{3,2,1,0:T(4,128)(2,1)} %copy.160), calls=%async_computation | async-start | bytes 1048576 | tf_op jit(solution)/shard_map/all_to_all | solution.py:138
  89.1 2.5 copy-start.2
  89.1 2.9 copy-start.4
  98.8 24.8 %all-to-all-start.3 = ((bf16[32,2,4,256]{3,2,1,0:T(4,128)(2,1)}), bf16[32,2,4,256]{3,2,1,0:T(4,128)(2,1)S(1)}, u32[]{:S(2)}, u32[]{:S(2)}) async-start(bf16[32,2,4,256]{3,2,1,0:T(4,128)(2,1)} %copy.173), calls=%async_computation.3 | async-start | bytes 262144 | tf_op jit(solution)/shard_map/all_to_all | solution.py:141
  123.7 10.9 %copy-start.5 = (bf16[2048,256]{1,0:T(8,128)(2,1)S(1)}, bf16[2048,256]{1,0:T(8,128)(2,1)}, u32[]{:S(2)}) copy-start(bf16[2048,256]{1,0:T(8,128)(2,1)} %param.10) | copy-start | bytes 3145732
  123.7 427.9 %all-to-all-start.2 = ((bf16[32,2,256,256]{3,2,1,0:T(8,128)(2,1)}), bf16[32,2,256,256]{3,2,1,0:T(8,128)(2,1)}, u32[]{:S(2)}, u32[]{:S(2)}) async-start(bf16[32,2,256,256]{3,2,1,0:T(8,128)(2,1)} %copy.164), calls=%async_computation.2 | async-start | bytes 16777216 | tf_op jit(solution)/shard_map/all_to_all | solution.py:135
  133.6 406.0 %all-reduce.2.cloned.1.call-start = ((), (), s32[]{:S(2)}) async-start(), calls=%async_computation.4 | async-start | bytes 2097152 | tf_op jit(solution)/shard_map/psum | solution.py:17
  568.0 8.3 %copy-start.3 = (f32[64,256,4,8]{1,3,2,0:T(8,128)S(1)}, f32[64,256,4,8]{1,3,2,0:T(8,128)}, u32[]{:S(2)}) copy-start(f32[64,256,4,8]{1,3,2,0:T(8,128)} %get-tuple-element.12) | copy-start | bytes 6291460
  577.6 3.8 copy-start.6
  581.4 10.5 %copy-start.1 = (bf16[8192,128]{1,0:T(8,128)(2,1)S(1)}, bf16[8192,128]{1,0:T(8,128)(2,1)}, u32[]{:S(2)}) copy-start(bf16[8192,128]{1,0:T(8,128)(2,1)} %param.18) | copy-start | bytes 6291460
Sparse Core Ops, SparseCore 0:
  10.0 58.4 all-gather.1
Sparse Core Ops, SparseCore 1:
  136.8 402.9 all-reduce.1
where the time goes:
time: 600 us; the launch traced here: 599 us
  waiting for transfers between devices  450 us (75%)
  matrix products  42 us (7%)
  starting transfers between devices  37.6 us (6%)
  local copies, waits for them, and re-layouts  35.5 us (6%)
  other arithmetic  18.5 us (3%)
  between operations  15.8 us (3%)
    psum x1, waiting for transfers between devices, broadcast(): return lax.psum(block, axis)  402 us
    all_gather x1, waiting for transfers between devices, per_device(): lax.all_gather(x_new, 'tensor', axis=2, tiled=True).astype(jnp.float32)  41.9 us
    dot_general x5, local copies, waits for them, and re-layouts, to_slots(): jnp.dot(selector, payload.reshape(row_count, -1), preferred_element_type=...  14.1 us
    all_to_all x1, starting transfers between devices, per_device(): lax.all_to_all(to_slots(request_lengths), 'dp', split_axis=0, concat_axis...  12.8 us
  transfers between devices with their start and end apart: 6, of which 3 were waited for; matrix products, arithmetic and copies ran while one was open for 9% of the time, Pallas kernels for 0%

commit v1 on v0

v1 whole, which is shorter than its diff:
```python
import math

import jax
import jax.numpy as jnp
from jax import lax
from jax.experimental import pallas as pl
from jax.experimental.pallas import tpu as pltpu
from jax.sharding import PartitionSpec as P

HEAD_SIZE = 128
CAP = 2
EPSILON = 1e-05
EXP_SCALE = math.log2(math.e) / math.sqrt(HEAD_SIZE)
VMEM_LIMIT = 40 * 1024 * 1024
Y, Z, CORE, X, PAIR = 4, 4, 2, 4, 2


def y_step(k):
    return [(i, (i + Z * CORE * k) % (Y * Z * CORE)) for i in range(Y * Z * CORE)]


def z_step(k):
    plane = Z * CORE
    return [(i, i // plane * plane + (i % plane + CORE * k) % plane) for i in range(Y * plane)]


def core_swap():
    return [(i, i ^ 1) for i in range(Y * Z * CORE)]


def x_step(k):
    return [(i, (i + PAIR * k) % (X * PAIR)) for i in range(X * PAIR)]


def pair_swap():
    return [(i, i ^ 1) for i in range(X * PAIR)]


def choose(index, options):
    chosen = options[0]
    for i in range(1, len(options)):
        chosen = jnp.where(index == i, options[i], chosen)
    return chosen


def dot_nt(a, b):
    return lax.dot_general(a, b, (((1,), (1,)), ((), ())), preferred_element_type=jnp.float32)


def with_ones(key_values):
    ones = jnp.ones((key_values.shape[0], HEAD_SIZE), key_values.dtype)
    return jnp.concatenate([ones, key_values[:, HEAD_SIZE:]], axis=1)


def weighted(scores, highest, key_values):
    weights = jnp.exp2(scores * EXP_SCALE - highest * EXP_SCALE).astype(jnp.bfloat16)
    return jnp.dot(weights, with_ones(key_values), preferred_element_type=jnp.float32)


def page_kernel(lengths, queries, pages, sums, tops):
    base = pl.program_id(0) * pages.shape[0]
    rows = queries.shape[0] // pages.shape[0]
    span = pages.shape[1]
    for i in range(pages.shape[0]):
        here = slice(i * rows, (i + 1) * rows)
        scores = dot_nt(queries[here, :], pages[i, :, :HEAD_SIZE])
        position = lax.broadcasted_iota(jnp.int32, (rows, span), 1)
        scores = jnp.where(position < lengths[base + i], scores, -jnp.inf)
        highest = jnp.max(scores, axis=1, keepdims=True)
        sums[here, :] = weighted(scores, highest, pages[i])
        tops[here, :] = highest


def page_part(lengths, queries, pages):
    count, span, width = pages.shape
    rows = queries.shape[0]
    batch = 4
    steps = count // batch
    return pl.pallas_call(
        page_kernel,
        grid_spec=pltpu.PrefetchScalarGridSpec(
            num_scalar_prefetch=1,
            grid=(steps,),
            in_specs=[
                pl.BlockSpec((rows // steps, HEAD_SIZE), lambda i, _: (i, 0)),
                pl.BlockSpec((batch, span, width), lambda i, _: (i, 0, 0)),
            ],
            out_specs=[
                pl.BlockSpec((rows // steps, 2 * HEAD_SIZE), lambda i, _: (i, 0)),
                pl.BlockSpec((rows // steps, 1), lambda i, _: (i, 0)),
            ],
        ),
        out_shape=[
            jax.ShapeDtypeStruct((rows, 2 * HEAD_SIZE), jnp.float32),
            jax.ShapeDtypeStruct((rows, 1), jnp.float32),
        ],
        compiler_params=pltpu.CompilerParams(vmem_limit_bytes=VMEM_LIMIT),
        cost_estimate=pl.CostEstimate(
            flops=4 * rows * span * HEAD_SIZE, bytes_accessed=pages.size * 2, transcendentals=rows * span
        ),
    )(lengths, queries, pages)


def prefix_kernel(queries, key_values, sums, tops):
    scores = dot_nt(queries[...], key_values[:, :HEAD_SIZE])
    highest = jnp.max(scores, axis=1, keepdims=True)
    sums[...] = weighted(scores, highest, key_values[...])
    tops[...] = highest


def prefix_part(queries, key_values):
    rows = queries.shape[0]
    span = key_values.shape[0]
    steps = 4
    return pl.pallas_call(
        prefix_kernel,
        grid=(steps,),
        in_specs=[
            pl.BlockSpec((rows // steps, HEAD_SIZE), lambda i: (i, 0)),
            pl.BlockSpec((span, 2 * HEAD_SIZE), lambda i: (0, 0)),
        ],
        out_specs=[
            pl.BlockSpec((rows // steps, 2 * HEAD_SIZE), lambda i: (i, 0)),
            pl.BlockSpec((rows // steps, 1), lambda i: (i, 0)),
        ],
        out_shape=[
            jax.ShapeDtypeStruct((rows, 2 * HEAD_SIZE), jnp.float32),
            jax.ShapeDtypeStruct((rows, 1), jnp.float32),
        ],
        compiler_params=pltpu.CompilerParams(vmem_limit_bytes=VMEM_LIMIT),
        cost_estimate=pl.CostEstimate(
            flops=8 * rows * span * HEAD_SIZE, bytes_accessed=span * 512, transcendentals=rows * span
        ),
    )(queries, key_values)


def projection_kernel(owners, gain, key_weight, value_weight, *refs):
    blocks, out = refs[:-1], refs[-1]
    wide = blocks[0].shape[1]
    tokens = blocks[0].shape[0]
    squares = jnp.zeros((tokens, 1), jnp.float32)
    for block in blocks:
        features = block[...].astype(jnp.float32)
        squares = squares + jnp.sum(features * features, axis=1, keepdims=True)
    scale = lax.rsqrt(squares / (wide * len(blocks)) + EPSILON)
    keys = jnp.zeros((tokens, HEAD_SIZE), jnp.float32)
    values = jnp.zeros((tokens, HEAD_SIZE), jnp.float32)
    for i, block in enumerate(blocks):
        normed = block[...].astype(jnp.float32) * scale * gain[pl.ds(owners[i], 1), :]
        normed = normed.astype(jnp.bfloat16)
        rows = pl.ds(pl.multiple_of(owners[i] * wide, wide), wide)
        keys = keys + jnp.dot(normed, key_weight[rows, :], preferred_element_type=jnp.float32)
        values = values + jnp.dot(normed, value_weight[rows, :], preferred_element_type=jnp.float32)
    out[:, :HEAD_SIZE] = keys.astype(jnp.bfloat16)
    out[:, HEAD_SIZE:] = values.astype(jnp.bfloat16)


def project(owners, gain, key_weight, value_weight, blocks):
    tokens, wide = blocks[0].shape
    vmem = pl.BlockSpec(memory_space=pltpu.VMEM)
    return pl.pallas_call(
        projection_kernel,
        in_specs=[pl.BlockSpec(memory_space=pltpu.SMEM)] + [vmem] * (3 + len(blocks)),
        out_specs=vmem,
        out_shape=jax.ShapeDtypeStruct((tokens, 2 * HEAD_SIZE), jnp.bfloat16),
        compiler_params=pltpu.CompilerParams(vmem_limit_bytes=VMEM_LIMIT),
        cost_estimate=pl.CostEstimate(
            flops=4 * tokens * key_weight.size, bytes_accessed=key_weight.size * 4, transcendentals=0
        ),
    )(owners, gain.reshape(len(blocks), wide), key_weight, value_weight, *blocks)


def merge_kernel(slots, queries, key_values, recent, *refs):
    parts, out = refs[:-1], refs[-1]
    rows = queries.shape[0]
    tokens = recent.shape[0]
    step = pl.program_id(0)
    requests = rows // 32

    @pl.when(step == 0)
    def _():
        out[...] = jnp.zeros_like(out)

    scores = dot_nt(queries[...], key_values[:, :HEAD_SIZE])
    new_scores = dot_nt(queries[...], recent[:, :HEAD_SIZE])
    row = lax.broadcasted_iota(jnp.int32, (rows, tokens), 0)
    token = lax.broadcasted_iota(jnp.int32, (rows, tokens), 1)
    seen = (row // 32 == token // 4) & (token % 4 <= (row % 32) // 8)
    new_scores = jnp.where(seen, new_scores, -jnp.inf)
    highest = jnp.maximum(
        jnp.max(scores, axis=1, keepdims=True), jnp.max(new_scores, axis=1, keepdims=True)
    )
    for top in parts[1::2]:
        highest = jnp.maximum(highest, top[...])
    total = weighted(scores, highest, key_values[...]) + weighted(new_scores, highest, recent[...])
    for sums, top in zip(parts[::2], parts[1::2]):
        total = total + sums[...] * jnp.exp2(top[...] * EXP_SCALE - highest * EXP_SCALE)
    result = (total[:, HEAD_SIZE:] / total[:, :HEAD_SIZE]).astype(jnp.bfloat16)
    for i in range(requests):
        out[slots[step * requests + i]] = result[i * 32 : (i + 1) * 32, :]


def merge(slots, queries, key_values, recent, parts, slot_count):
    rows = queries.shape[0]
    span = key_values.shape[0]
    steps = 4
    part_specs = []
    for part in parts:
        part_specs.append(pl.BlockSpec((rows // steps, part.shape[1]), lambda i, _: (i, 0)))
    return pl.pallas_call(
        merge_kernel,
        grid_spec=pltpu.PrefetchScalarGridSpec(
            num_scalar_prefetch=1,
            grid=(steps,),
            in_specs=[
                pl.BlockSpec((rows // steps, HEAD_SIZE), lambda i, _: (i, 0)),
                pl.BlockSpec((span, 2 * HEAD_SIZE), lambda i, _: (0, 0)),
                pl.BlockSpec((recent.shape[0] // steps, 2 * HEAD_SIZE), lambda i, _: (i, 0)),
            ]
            + part_specs,
            out_specs=pl.BlockSpec((slot_count, 32, HEAD_SIZE), lambda i, _: (0, 0, 0)),
        ),
        out_shape=jax.ShapeDtypeStruct((slot_count, 32, HEAD_SIZE), jnp.bfloat16),
        compiler_params=pltpu.CompilerParams(vmem_limit_bytes=VMEM_LIMIT),
        cost_estimate=pl.CostEstimate(
            flops=8 * rows * span * HEAD_SIZE, bytes_accessed=span * 512, transcendentals=rows * span
        ),
    )(slots, queries, key_values, recent, *parts)


def gather_features(block):
    me = lax.axis_index("tensor")
    x, pair = me // PAIR, me % PAIR
    half = block.shape[0] // 2
    twin = lax.ppermute(block, "tensor", pair_swap())
    left = lax.ppermute(block, "tensor", x_step(1))
    right = lax.ppermute(block, "tensor", x_step(X - 1))
    far_top = lax.ppermute(left[:half], "tensor", x_step(1))
    far_bottom = lax.ppermute(right[half:], "tensor", x_step(X - 1))
    twin_left = lax.ppermute(twin, "tensor", x_step(1))
    twin_right = lax.ppermute(twin, "tensor", x_step(X - 1))
    far = jnp.concatenate([far_top, far_bottom])
    twin_far = lax.ppermute(far, "tensor", pair_swap())
    places = [(0, 0), (0, 1), (X - 1, 0), (1, 0), (X - 1, 1), (1, 1), (2, 0), (2, 1)]
    owners = jnp.stack([(x + dx) % X * PAIR + (pair ^ flip) for dx, flip in places])
    return owners.astype(jnp.int32), [block, twin, left, right, twin_left, twin_right, far, twin_far]


def spread_prefix(block, owner):
    me = lax.axis_index("dp")
    y, z, core = me // (Z * CORE), me // CORE % Z, me % CORE
    own_y, own_z, own_core = owner // (Z * CORE), owner // CORE % Z, owner % CORE
    half = block.shape[0] // 2
    piece = half // Y
    other = lax.ppermute(block[half:], "dp", core_swap())
    mine = jnp.where(core == own_core, block[:half], other)
    arrived = [mine[:piece]]
    for k in range(1, Y):
        arrived.append(lax.ppermute(mine[piece * k : piece * (k + 1)], "dp", y_step(k)))
    part = choose((y - own_y) % Y, arrived)
    part = choose((z - own_z) % Z, [part] + [lax.ppermute(part, "dp", z_step(k)) for k in range(1, Z)])
    near = jnp.concatenate([part] + [lax.ppermute(part, "dp", y_step(k)) for k in range(1, Y)])
    return near, lax.ppermute(near, "dp", core_swap())


def per_device(
    prefix_kv,
    page_key_values,
    context_len,
    prefill_owner,
    assign,
    x_new,
    norm_gain,
    key_weight,
    value_weight,
    decoded_queries,
):
    row_count, step_count, width = decoded_queries.shape
    group_count = lax.axis_size("dp")
    near, far = spread_prefix(prefix_kv, prefill_owner[0])
    owners, blocks = gather_features(x_new.reshape(row_count * step_count, x_new.shape[2]))

    assigned = assign[:, 0]
    indices = jnp.arange(row_count)
    matching = (assigned[:, None] == assigned[None, :]) & (indices[None, :] < indices[:, None])
    slots = assigned * CAP + jnp.sum(matching.astype(jnp.int32), axis=1)

    queries = decoded_queries.reshape(-1, HEAD_SIZE)
    page_sums, page_tops = page_part(context_len, queries, page_key_values)
    recent = project(owners, norm_gain, key_weight, value_weight, blocks)
    near_sums, near_tops = prefix_part(queries, near)
    slot_count = group_count * CAP
    result = merge(
        slots, queries, far, recent, [page_sums, page_tops, near_sums, near_tops], slot_count
    )
    decoded = lax.all_to_all(
        result.reshape(group_count, CAP * 32, HEAD_SIZE), "dp", split_axis=0, concat_axis=0, tiled=True
    )
    return decoded.reshape(slot_count, step_count, width)


def solution(mesh):
    in_specs = (
        P("dp", "tensor"),
        P("dp", None, "tensor"),
        P("dp"),
        P(),
        P("dp", None),
        P("dp", None, "tensor"),
        P(),
        P(None, "tensor"),
        P(None, "tensor"),
        P("dp", None, "tensor"),
    )
    out_specs = P("dp", None, "tensor")
    return jax.shard_map(
        per_device, mesh=mesh, in_specs=in_specs, out_specs=out_specs, check_vma=False
    )
```

time: 600 us -> 95.3 us (0.16)
  waiting for transfers between devices: 450 us -> 15.5 us
  matrix products: 42 us -> 0 us
  local copies, waits for them, and re-layouts: 35.5 us -> 5.53 us
  blocking collectives: 0 us -> 26.6 us
  other arithmetic: 18.5 us -> 1.4 us
  Pallas kernels: 0 us -> 15.1 us
  between operations: 15.8 us -> 0.96 us
  starting transfers between devices: 37.6 us -> 29.9 us
    psum x1 -> x0, waiting for transfers between devices: 402 us -> none  [broadcast(): return lax.psum(block, axis)]
    dot_general x12 -> x0, matrix products: 42 us -> none  [the longest x4 10.7 us: to_slots(): jnp.dot(selector, payload.reshape(row_count, -1), preferred_element_type=...]
    all_gather x1 -> x0, waiting for transfers between devices: 41.9 us -> none  [per_device(): lax.all_gather(x_new, 'tensor', axis=2, tiled=True).astype(jnp.float32)]
    all_to_all x4 -> x0, starting transfers between devices: 37.3 us -> none  [the longest x1 12.8 us: per_device(): lax.all_to_all(to_slots(request_lengths), 'dp', split_axis=0, concat_axis...]
    ppermute x0 -> x19, starting transfers between devices: none -> 29.9 us  [the longest x3 9.8 us: spread_prefix(): lax.ppermute(part, 'dp', z_step(k))]
    all_to_all x0 -> x1, blocking collectives: none -> 26.6 us  [per_device(): lax.all_to_all(result.reshape(group_count, CAP * 32, HEAD_SIZE), 'dp', sp...]
    ppermute x0 -> x19, waiting for transfers between devices: none -> 15.5 us  [the longest x3 6.12 us: spread_prefix(): lax.ppermute(part, 'dp', z_step(k))]
    pallas_call x0 -> x4, Pallas kernels: none -> 15.1 us  [the longest x1 5.17 us: merge(): pl.pallas_call(merge_kernel, grid_spec=pltpu.PrefetchScalarGridSpec(num_s...]
  transfers between devices with their start and end apart: 6 -> 19, of which waited for: 3 -> 8; matrix products, arithmetic and copies ran while one was open for 9% -> 2% of each run, Pallas kernels for 0% -> 10%
where the time goes in v1:
time: 95.3 us; the launch traced here: 95 us
  starting transfers between devices  29.9 us (31%)
  blocking collectives  26.6 us (28%)
  waiting for transfers between devices  15.5 us (16%)
  Pallas kernels  15.1 us (16%)
  local copies, waits for them, and re-layouts  5.53 us (6%)
  other arithmetic  1.4 us (1%)
  between operations  0.96 us (1%)
    all_to_all x1, blocking collectives, per_device(): lax.all_to_all(result.reshape(group_count, CAP * 32, HEAD_SIZE), 'dp', sp...  26.6 us
    ppermute x3, starting transfers between devices, spread_prefix(): lax.ppermute(part, 'dp', z_step(k))  9.8 us
    ppermute x3, waiting for transfers between devices, spread_prefix(): lax.ppermute(part, 'dp', z_step(k))  6.12 us
    pallas_call x1, Pallas kernels, merge(): pl.pallas_call(merge_kernel, grid_spec=pltpu.PrefetchScalarGridSpec(num_s...  5.17 us
    ppermute x3, waiting for transfers between devices, spread_prefix(): lax.ppermute(mine[piece * k:piece * (k + 1)], 'dp', y_step(k))  4.38 us
    pallas_call x1, Pallas kernels, page_part(): pl.pallas_call(page_kernel, grid_spec=pltpu.PrefetchScalarGridSpec(num_sc...  4.21 us
    pallas_call x1, Pallas kernels, prefix_part(): pl.pallas_call(prefix_kernel, grid=(steps,), in_specs=[pl.BlockSpec((rows...  3.39 us
    ppermute x1, starting transfers between devices, spread_prefix(): other = lax.ppermute(block[half:], 'dp', core_swap())  3.33 us
  transfers between devices with their start and end apart: 19, of which 8 were waited for; matrix products, arithmetic and copies ran while one was open for 2% of the time, Pallas kernels for 10%

profile of v1, /device:TPU:1, one launch (start us, length us, event | category | flops | bytes accessed | tf_op | source)
XLA Modules:
  0.0 95.0 jit_solution(3084036729466493216)
XLA Ops:
  0.0 0.0 copy-start.4
  0.0 1.1 %slice.25 = bf16[1024,256]{1,0:T(8,128)(2,1)S(1)} slice(bf16[2048,256]{1,0:T(8,128)(2,1)} %param.10), slice={[1024:2048], [0:256]} | slice | bytes 1048576 | tf_op jit(solution)/shard_map/slice | solution.py:255
  1.1 3.3 %collective-permute-start = (bf16[1024,256]{1,0:T(8,128)(2,1)S(1)}, bf16[1024,256]{1,0:T(8,128)(2,1)S(1)}, u32[]{:S(2)}, u32[]{:S(2)}) collective-permute-start(bf16[1024,256]{1,0:T(8,128)(2,1)S(1)} %slice.25), channel_id=1, source_target_pairs={{0,8},{8,0},{16,24},{24,16},{32,40},{40,32},{48,56},{56,48},{64,72... | collective-permute-start | bytes 1572872 | tf_op jit(solution)/shard_map/ppermute | solution.py:255
  5.1 0.9 collective-permute-done
  6.0 1.1 %slice_select_fusion = bf16[1024,256]{1,0:T(8,128)(2,1)S(1)} fusion(bf16[1024,256]{1,0:T(8,128)(2,1)S(1)} %collective-permute-done, bf16[2048,256]{1,0:T(8,128)(2,1)} %param.10, pred[]{:T(512)S(6)} %eq.55), kind=kLoop, calls=%fused_computation.1 | loop fusion | flops 262144 | bytes 1572865 | tf_op jit(solution)/shard_map/jit(_where)/select_n | solution.py:256
  7.2 0.0 copy-start.6
  7.2 0.1 collective-permute-start.3
  7.3 2.2 %collective-permute-start.2 = (bf16[256,256]{1,0:T(8,128)(2,1)S(1)}, bf16[256,256]{1,0:T(8,128)(2,1)S(1)}, u32[]{:S(2)}, u32[]{:S(2)}) collective-permute-start(bf16[256,256]{1,0:T(8,128)(2,1)S(1)} %get-tuple-element.14), channel_id=1, source_target_pairs={{0,128},{8,136},{16,144},{24,152},{32,160},{40,168},{48,176},{56,1... | collective-permute-start | bytes 393224 | tf_op jit(solution)/shard_map/ppermute | solution.py:259
  9.4 0.0 copy-start.5
  9.4 1.1 %collective-permute-start.1 = (bf16[256,256]{1,0:T(8,128)(2,1)S(1)}, bf16[256,256]{1,0:T(8,128)(2,1)S(1)}, u32[]{:S(2)}, u32[]{:S(2)}) collective-permute-start(bf16[256,256]{1,0:T(8,128)(2,1)S(1)} %get-tuple-element.15), channel_id=1, source_target_pairs={{0,192},{8,200},{16,208},{24,216},{32,224},{40,232},{48,240},{56,2... | collective-permute-start | bytes 393224 | tf_op jit(solution)/shard_map/ppermute | solution.py:259
  10.5 0.0 copy-done.4
  10.5 0.1 reshape.18.refs_0_
  10.6 1.3 %collective-permute-start.12 = (bf16[128,1024]{1,0:T(8,128)(2,1)S(1)}, bf16[128,1024]{1,0:T(8,128)(2,1)S(1)}, u32[]{:S(2)}, u32[]{:S(2)}) collective-permute-start(bf16[128,1024]{1,0:T(8,128)(2,1)S(1)} %reshape.18.refs_0_), channel_id=1, source_target_pairs={{0,2},{1,3},{2,4},{3,5},{4,6},{5,7},{6,0},{7,1},{8,10},{9,11},{10,... | collective-permute-start | bytes 786440 | tf_op jit(solution)/shard_map/ppermute | solution.py:236
  11.9 0.0 copy-start.3
  11.9 1.8 %collective-permute-done.3 = bf16[256,256]{1,0:T(8,128)(2,1)S(1)} collective-permute-done((bf16[256,256]{1,0:T(8,128)(2,1)S(1)}, bf16[256,256]{1,0:T(8,128)(2,1)S(1)}, u32[]{:S(2)}, u32[]{:S(2)}) %collective-permute-start.3) | collective-permute-done | bytes 131104 | tf_op jit(solution)/shard_map/ppermute | solution.py:259
  13.7 1.9 %collective-permute-done.2 = bf16[256,256]{1,0:T(8,128)(2,1)S(1)} collective-permute-done((bf16[256,256]{1,0:T(8,128)(2,1)S(1)}, bf16[256,256]{1,0:T(8,128)(2,1)S(1)}, u32[]{:S(2)}, u32[]{:S(2)}) %collective-permute-start.2) | collective-permute-done | bytes 131104 | tf_op jit(solution)/shard_map/ppermute | solution.py:259
  15.5 0.7 collective-permute-done.1
  16.3 2.3 %collective-permute-start.6 = (bf16[256,256]{1,0:T(8,128)(2,1)S(1)}, bf16[256,256]{1,0:T(8,128)(2,1)S(1)}, u32[]{:S(2)}, u32[]{:S(2)}) collective-permute-start(bf16[256,256]{1,0:T(8,128)(2,1)S(1)} %fusion.1), channel_id=1, source_target_pairs={{0,16},{8,24},{16,32},{24,40},{32,48},{40,56},{48,0},{56,8},{64,80... | collective-permute-start | bytes 393224 | tf_op jit(solution)/shard_map/ppermute | solution.py:261
  18.6 5.1 %collective-permute-start.5 = (bf16[256,256]{1,0:T(8,128)(2,1)S(1)}, bf16[256,256]{1,0:T(8,128)(2,1)S(1)}, u32[]{:S(2)}, u32[]{:S(2)}) collective-permute-start(bf16[256,256]{1,0:T(8,128)(2,1)S(1)} %fusion.1), channel_id=1, source_target_pairs={{0,32},{8,40},{16,48},{24,56},{32,0},{40,8},{48,16},{56,24},{64,96... | collective-permute-start | bytes 393224 | tf_op jit(solution)/shard_map/ppermute | solution.py:261
  23.7 2.4 %collective-permute-start.4 = (bf16[256,256]{1,0:T(8,128)(2,1)S(1)}, bf16[256,256]{1,0:T(8,128)(2,1)S(1)}, u32[]{:S(2)}, u32[]{:S(2)}) collective-permute-start(bf16[256,256]{1,0:T(8,128)(2,1)S(1)} %fusion.1), channel_id=1, source_target_pairs={{0,48},{8,56},{16,0},{24,8},{32,16},{40,24},{48,32},{56,40},{64,11... | collective-permute-start | bytes 393224 | tf_op jit(solution)/shard_map/ppermute | solution.py:261
  26.1 2.5 %collective-permute-start.13 = (bf16[128,1024]{1,0:T(8,128)(2,1)S(1)}, bf16[128,1024]{1,0:T(8,128)(2,1)S(1)}, u32[]{:S(2)}, u32[]{:S(2)}) collective-permute-start(bf16[128,1024]{1,0:T(8,128)(2,1)S(1)} %reshape.18.refs_0_), channel_id=1, source_target_pairs={{0,6},{1,7},{2,0},{3,1},{4,2},{5,3},{6,4},{7,5},{8,14},{9,15},{10,... | collective-permute-start | bytes 786440 | tf_op jit(solution)/shard_map/ppermute | solution.py:237
  28.6 0.0 collective-permute-done.12.refs_2_
  28.6 0.7 collective-permute-start.11
  29.3 0.0 collective-permute-done.6
  29.3 0.1 collective-permute-start.16
  29.4 1.9 %collective-permute-done.5 = bf16[256,256]{1,0:T(8,128)(2,1)S(1)} collective-permute-done((bf16[256,256]{1,0:T(8,128)(2,1)S(1)}, bf16[256,256]{1,0:T(8,128)(2,1)S(1)}, u32[]{:S(2)}, u32[]{:S(2)}) %collective-permute-start.5) | collective-permute-done | bytes 131104 | tf_op jit(solution)/shard_map/ppermute | solution.py:261
  31.3 4.2 %collective-permute-done.4 = bf16[256,256]{1,0:T(8,128)(2,1)S(1)} collective-permute-done((bf16[256,256]{1,0:T(8,128)(2,1)S(1)}, bf16[256,256]{1,0:T(8,128)(2,1)S(1)}, u32[]{:S(2)}, u32[]{:S(2)}) %collective-permute-start.4) | collective-permute-done | bytes 131104 | tf_op jit(solution)/shard_map/ppermute | solution.py:261
  35.6 2.6 %collective-permute-start.9 = (bf16[256,256]{1,0:T(8,128)(2,1)S(1)}, bf16[256,256]{1,0:T(8,128)(2,1)S(1)}, u32[]{:S(2)}, u32[]{:S(2)}) collective-permute-start(bf16[256,256]{1,0:T(8,128)(2,1)S(1)} %select_select_fusion), channel_id=1, source_target_pairs={{0,192},{8,200},{16,208},{24,216},{32,224},{40,232},{48,240},{56,2... | collective-permute-start | bytes 393224 | tf_op jit(solution)/shard_map/ppermute | solution.py:262
  38.2 0.2 collective-permute-start.8
  38.3 0.0 collective-permute-done.13.refs_3_
  38.3 0.5 collective-permute-start.7
  38.9 2.5 %collective-permute-done.11.refs_1_ = bf16[128,1024]{1,0:T(8,128)(2,1)S(1)} collective-permute-done((bf16[128,1024]{1,0:T(8,128)(2,1)S(1)}, bf16[128,1024]{1,0:T(8,128)(2,1)S(1)}, u32[]{:S(2)}, u32[]{:S(2)}) %collective-permute-start.11) | collective-permute-done | bytes 262176 | tf_op jit(solution)/shard_map/ppermute | solution.py:235
  41.3 2.5 %collective-permute-start.17 = (bf16[64,1024]{1,0:T(8,128)(2,1)S(1)}, bf16[64,1024]{1,0:T(8,128)(2,1)S(1)}, u32[]{:S(2)}, u32[]{:S(2)}) collective-permute-start(bf16[64,1024]{1,0:T(8,128)(2,1)S(1)} %slice.37), channel_id=1, source_target_pairs={{0,6},{1,7},{2,0},{3,1},{4,2},{5,3},{6,4},{7,5},{8,14},{9,15},{10,... | collective-permute-start | bytes 393224 | tf_op jit(solution)/shard_map/ppermute | solution.py:239
  43.8 0.0 collective-permute-done.16
  43.8 0.5 collective-permute-start.15
  44.4 0.0 collective-permute-done.9
  44.4 1.2 %collective-permute-start.14 = (bf16[128,1024]{1,0:T(8,128)(2,1)S(1)}, bf16[128,1024]{1,0:T(8,128)(2,1)S(1)}, u32[]{:S(2)}, u32[]{:S(2)}) collective-permute-start(bf16[128,1024]{1,0:T(8,128)(2,1)S(1)} %collective-permute-done.11.refs_1_), channel_id=1, source_target_pairs={{0,2},{1,3},{2,4},{3,5},{4,6},{5,7},{6,0},{7,1},{8,10},{9,11},{10,... | collective-permute-start | bytes 786440 | tf_op jit(solution)/shard_map/ppermute | solution.py:240
  45.6 0.0 collective-permute-done.8
  45.6 1.7 %collective-permute-done.7 = bf16[256,256]{1,0:T(8,128)(2,1)S(1)} collective-permute-done((bf16[256,256]{1,0:T(8,128)(2,1)S(1)}, bf16[256,256]{1,0:T(8,128)(2,1)S(1)}, u32[]{:S(2)}, u32[]{:S(2)}) %collective-permute-start.7) | collective-permute-done | bytes 131104 | tf_op jit(solution)/shard_map/ppermute | solution.py:262
  47.3 1.1 %collective-permute-start.10 = (bf16[1024,256]{1,0:T(8,128)(2,1)S(1)}, bf16[1024,256]{1,0:T(8,128)(2,1)S(1)}, u32[]{:S(2)}, u32[]{:S(2)}) collective-permute-start(bf16[1024,256]{1,0:T(8,128)(2,1)S(1)} %pad_maximum_fusion.key_values), channel_id=1, source_target_pairs={{0,8},{8,0},{16,24},{24,16},{32,40},{40,32},{48,56},{56,48},{64,72... | collective-permute-start | bytes 1572872 | tf_op jit(solution)/shard_map/ppermute | solution.py:263
  48.4 0.0 collective-permute-done.17
  48.4 0.2 collective-permute-start.18
  48.6 0.0 copy-done.6
  48.6 0.2 convert_reduce_fusion
  48.9 0.0 copy-done.5
  48.9 1.1 %reshape.16.queries = bf16[1024,128]{1,0:T(8,128)(2,1)S(1)} reshape(bf16[32,4,1024]{2,1,0:T(4,128)(2,1)} %param.19) | data formatting | bytes 524288 | tf_op jit(solution)/shard_map/reshape | solution.py:288
  50.0 0.1 stack.35.owners
  50.1 0.0 copy-done.3
  50.1 0.0 copy-start
  50.1 2.2 %copy-done = bf16[32,256,256]{2,1,0:T(8,128)(2,1)S(1)} copy-done((bf16[32,256,256]{2,1,0:T(8,128)(2,1)S(1)}, bf16[32,256,256]{2,1,0:T(8,128)(2,1)}, u32[]{:S(2)}) %copy-start) | copy-done | bytes 4194328
  52.3 0.0 copy-start.1
  52.3 0.0 copy-start.2
  52.3 4.2 %shard_map.101 = (f32[1024,256]{1,0:T(8,128)S(1)}, f32[1024,1]{1,0:T(8,128)S(1)}) custom-call(s32[32]{0:T(128)S(1)} %copy-done.3, bf16[1024,128]{1,0:T(8,128)(2,1)S(1)} %reshape.16.queries, bf16[32,256,256]{2,1,0:T(8,128)(2,1)S(1)} %copy-done), custom_call_target="tpu_custom_call" | custom-call | flops 134217728 | bytes 4194304 | tf_op jit(solution)/shard_map/pallas_call | solution.py:79
  56.5 0.0 collective-permute-done.15.refs_5_
  56.5 0.0 collective-permute-done.14.refs_4_
  56.5 0.0 collective-permute-done.18.refs_7_
  56.5 0.0 copy-done.1
  56.5 0.0 copy-done.2
  56.5 2.3 %shard_map.100.recent = bf16[128,256]{1,0:T(8,128)(2,1)S(1)} custom-call(s32[8]{0:T(128)S(1)} %stack.35.owners, f32[8,1024]{1,0:T(8,128)S(1)} %reshape.17.gain, bf16[8192,128]{1,0:T(8,128)(2,1)S(1)} %copy-done.1, bf16[8192,128]{1,0:T(8,128)(2,1)S(1)} %copy-done.2, bf16[128,1024]{1,0:T(8,128)(2,1)S(1)} %reshape.18.refs_0_, ...), custom_call_target="tpu_custom_call" | custom-call | flops 536870912 | bytes 4194304 | tf_op jit(solution)/shard_map/pallas_call | solution.py:161
  58.9 3.4 %shard_map.102 = (f32[1024,256]{1,0:T(8,128)S(1)}, f32[1024,1]{1,0:T(8,128)S(1)}) custom-call(bf16[1024,128]{1,0:T(8,128)(2,1)S(1)} %reshape.16.queries, bf16[1024,256]{1,0:T(8,128)(2,1)S(1)} %pad_maximum_fusion.key_values), custom_call_target="tpu_custom_call" | custom-call | flops 1073741824 | bytes 524288 | tf_op jit(solution)/shard_map/pallas_call | solution.py:115
  62.3 0.0 collective-permute-done.10.key_values
  62.3 5.2 %shard_map.103 = bf16[64,32,128]{2,1,0:T(8,128)(2,1)S(1)} custom-call(s32[32]{0:T(128)S(1)} %multiply_add_fusion.slots, bf16[1024,128]{1,0:T(8,128)(2,1)S(1)} %reshape.16.queries, bf16[1024,256]{1,0:T(8,128)(2,1)S(1)} %collective-permute-done.10.key_values, bf16[128,256]{1,0:T(8,128)(2,1)S(1)} %shard_map.100.recent, ...), custom_call_target="tpu_custom_call" | custom-call | flops 1073741824 | bytes 524288 | tf_op jit(solution)/shard_map/pallas_call | solution.py:210
  67.4 26.6 %all_to_all.5 = bf16[32,64,128]{2,1,0:T(8,128)(2,1)S(1)} all-to-all(bf16[32,64,128]{2,1,0:T(8,128)(2,1)S(1)} %bitcast.16), channel_id=1, replica_groups=mesh['dp'=32,'tensor'=8] {'dp'}, dimensions={0} | all-to-all | bytes 1048576 | tf_op jit(solution)/shard_map/all_to_all | solution.py:296
  94.1 0.9 reshape.20
  (10 shorter events, 0.2 us)
Async XLA Ops:
  0.0 10.5 %copy-start.4 = (bf16[32,4,1024]{2,1,0:T(4,128)(2,1)S(1)}, bf16[32,4,1024]{2,1,0:T(4,128)(2,1)}, u32[]{:S(2)}) copy-start(bf16[32,4,1024]{2,1,0:T(4,128)(2,1)} %param.15) | copy-start | bytes 786436
  1.1 4.9 %collective-permute-start = (bf16[1024,256]{1,0:T(8,128)(2,1)S(1)}, bf16[1024,256]{1,0:T(8,128)(2,1)S(1)}, u32[]{:S(2)}, u32[]{:S(2)}) collective-permute-start(bf16[1024,256]{1,0:T(8,128)(2,1)S(1)} %slice.25), channel_id=1, source_target_pairs={{0,8},{8,0},{16,24},{24,16},{32,40},{40,32},{48,56},{56,48},{64,72... | collective-permute-start | bytes 1572872 | tf_op jit(solution)/shard_map/ppermute | solution.py:255
  7.2 41.5 %copy-start.6 = (s32[32,1]{0,1:T(1,128)S(1)}, s32[32,1]{0,1:T(1,128)}, u32[]{:S(2)}) copy-start(s32[32,1]{0,1:T(1,128)} %param.14) | copy-start | bytes 388
  7.2 6.5 %collective-permute-start.3 = (bf16[256,256]{1,0:T(8,128)(2,1)S(1)}, bf16[256,256]{1,0:T(8,128)(2,1)S(1)}, u32[]{:S(2)}, u32[]{:S(2)}) collective-permute-start(bf16[256,256]{1,0:T(8,128)(2,1)S(1)} %get-tuple-element.13), channel_id=1, source_target_pairs={{0,64},{8,72},{16,80},{24,88},{32,96},{40,104},{48,112},{56,120},{... | collective-permute-start | bytes 393224 | tf_op jit(solution)/shard_map/ppermute | solution.py:259
  7.3 8.3 %collective-permute-start.2 = (bf16[256,256]{1,0:T(8,128)(2,1)S(1)}, bf16[256,256]{1,0:T(8,128)(2,1)S(1)}, u32[]{:S(2)}, u32[]{:S(2)}) collective-permute-start(bf16[256,256]{1,0:T(8,128)(2,1)S(1)} %get-tuple-element.14), channel_id=1, source_target_pairs={{0,128},{8,136},{16,144},{24,152},{32,160},{40,168},{48,176},{56,1... | collective-permute-start | bytes 393224 | tf_op jit(solution)/shard_map/ppermute | solution.py:259
  9.4 39.5 %copy-start.5 = (f32[8192]{0:T(1024)S(1)}, f32[8192]{0:T(1024)}, u32[]{:S(2)}) copy-start(f32[8192]{0:T(1024)} %param.16) | copy-start | bytes 98308
  9.4 6.8 %collective-permute-start.1 = (bf16[256,256]{1,0:T(8,128)(2,1)S(1)}, bf16[256,256]{1,0:T(8,128)(2,1)S(1)}, u32[]{:S(2)}, u32[]{:S(2)}) collective-permute-start(bf16[256,256]{1,0:T(8,128)(2,1)S(1)} %get-tuple-element.15), channel_id=1, source_target_pairs={{0,192},{8,200},{16,208},{24,216},{32,224},{40,232},{48,240},{56,2... | collective-permute-start | bytes 393224 | tf_op jit(solution)/shard_map/ppermute | solution.py:259
  10.6 18.0 %collective-permute-start.12 = (bf16[128,1024]{1,0:T(8,128)(2,1)S(1)}, bf16[128,1024]{1,0:T(8,128)(2,1)S(1)}, u32[]{:S(2)}, u32[]{:S(2)}) collective-permute-start(bf16[128,1024]{1,0:T(8,128)(2,1)S(1)} %reshape.18.refs_0_), channel_id=1, source_target_pairs={{0,2},{1,3},{2,4},{3,5},{4,6},{5,7},{6,0},{7,1},{8,10},{9,11},{10,... | collective-permute-start | bytes 786440 | tf_op jit(solution)/shard_map/ppermute | solution.py:236
  11.9 38.2 %copy-start.3 = (s32[32]{0:T(128)S(1)}, s32[32]{0:T(128)}, u32[]{:S(2)}) copy-start(s32[32]{0:T(128)} %lengths.1) | copy-start | bytes 388
  16.3 13.0 %collective-permute-start.6 = (bf16[256,256]{1,0:T(8,128)(2,1)S(1)}, bf16[256,256]{1,0:T(8,128)(2,1)S(1)}, u32[]{:S(2)}, u32[]{:S(2)}) collective-permute-start(bf16[256,256]{1,0:T(8,128)(2,1)S(1)} %fusion.1), channel_id=1, source_target_pairs={{0,16},{8,24},{16,32},{24,40},{32,48},{40,56},{48,0},{56,8},{64,80... | collective-permute-start | bytes 393224 | tf_op jit(solution)/shard_map/ppermute | solution.py:261
  18.6 12.7 %collective-permute-start.5 = (bf16[256,256]{1,0:T(8,128)(2,1)S(1)}, bf16[256,256]{1,0:T(8,128)(2,1)S(1)}, u32[]{:S(2)}, u32[]{:S(2)}) collective-permute-start(bf16[256,256]{1,0:T(8,128)(2,1)S(1)} %fusion.1), channel_id=1, source_target_pairs={{0,32},{8,40},{16,48},{24,56},{32,0},{40,8},{48,16},{56,24},{64,96... | collective-permute-start | bytes 393224 | tf_op jit(solution)/shard_map/ppermute | solution.py:261
  23.7 11.8 %collective-permute-start.4 = (bf16[256,256]{1,0:T(8,128)(2,1)S(1)}, bf16[256,256]{1,0:T(8,128)(2,1)S(1)}, u32[]{:S(2)}, u32[]{:S(2)}) collective-permute-start(bf16[256,256]{1,0:T(8,128)(2,1)S(1)} %fusion.1), channel_id=1, source_target_pairs={{0,48},{8,56},{16,0},{24,8},{32,16},{40,24},{48,32},{56,40},{64,11... | collective-permute-start | bytes 393224 | tf_op jit(solution)/shard_map/ppermute | solution.py:261
  26.1 12.3 %collective-permute-start.13 = (bf16[128,1024]{1,0:T(8,128)(2,1)S(1)}, bf16[128,1024]{1,0:T(8,128)(2,1)S(1)}, u32[]{:S(2)}, u32[]{:S(2)}) collective-permute-start(bf16[128,1024]{1,0:T(8,128)(2,1)S(1)} %reshape.18.refs_0_), channel_id=1, source_target_pairs={{0,6},{1,7},{2,0},{3,1},{4,2},{5,3},{6,4},{7,5},{8,14},{9,15},{10,... | collective-permute-start | bytes 786440 | tf_op jit(solution)/shard_map/ppermute | solution.py:237
  28.6 12.8 %collective-permute-start.11 = (bf16[128,1024]{1,0:T(8,128)(2,1)S(1)}, bf16[128,1024]{1,0:T(8,128)(2,1)S(1)}, u32[]{:S(2)}, u32[]{:S(2)}) collective-permute-start(bf16[128,1024]{1,0:T(8,128)(2,1)S(1)} %reshape.18.refs_0_), channel_id=1, source_target_pairs={{0,1},{1,0},{2,3},{3,2},{4,5},{5,4},{6,7},{7,6},{8,9},{9,8},{10,11... | collective-permute-start | bytes 786440 | tf_op jit(solution)/shard_map/ppermute | solution.py:235
  29.3 14.5 %collective-permute-start.16 = (bf16[64,1024]{1,0:T(8,128)(2,1)S(1)}, bf16[64,1024]{1,0:T(8,128)(2,1)S(1)}, u32[]{:S(2)}, u32[]{:S(2)}) collective-permute-start(bf16[64,1024]{1,0:T(8,128)(2,1)S(1)} %slice.36), channel_id=1, source_target_pairs={{0,2},{1,3},{2,4},{3,5},{4,6},{5,7},{6,0},{7,1},{8,10},{9,11},{10,... | collective-permute-start | bytes 393224 | tf_op jit(solution)/shard_map/ppermute | solution.py:238
  35.6 8.8 %collective-permute-start.9 = (bf16[256,256]{1,0:T(8,128)(2,1)S(1)}, bf16[256,256]{1,0:T(8,128)(2,1)S(1)}, u32[]{:S(2)}, u32[]{:S(2)}) collective-permute-start(bf16[256,256]{1,0:T(8,128)(2,1)S(1)} %select_select_fusion), channel_id=1, source_target_pairs={{0,192},{8,200},{16,208},{24,216},{32,224},{40,232},{48,240},{56,2... | collective-permute-start | bytes 393224 | tf_op jit(solution)/shard_map/ppermute | solution.py:262
  38.2 7.4 %collective-permute-start.8 = (bf16[256,256]{1,0:T(8,128)(2,1)S(1)}, bf16[256,256]{1,0:T(8,128)(2,1)S(1)}, u32[]{:S(2)}, u32[]{:S(2)}) collective-permute-start(bf16[256,256]{1,0:T(8,128)(2,1)S(1)} %select_select_fusion), channel_id=1, source_target_pairs={{0,128},{8,136},{16,144},{24,152},{32,160},{40,168},{48,176},{56,1... | collective-permute-start | bytes 393224 | tf_op jit(solution)/shard_map/ppermute | solution.py:262
  38.3 8.9 %collective-permute-start.7 = (bf16[256,256]{1,0:T(8,128)(2,1)S(1)}, bf16[256,256]{1,0:T(8,128)(2,1)S(1)}, u32[]{:S(2)}, u32[]{:S(2)}) collective-permute-start(bf16[256,256]{1,0:T(8,128)(2,1)S(1)} %select_select_fusion), channel_id=1, source_target_pairs={{0,64},{8,72},{16,80},{24,88},{32,96},{40,104},{48,112},{56,120},{... | collective-permute-start | bytes 393224 | tf_op jit(solution)/shard_map/ppermute | solution.py:262
  41.3 7.1 %collective-permute-start.17 = (bf16[64,1024]{1,0:T(8,128)(2,1)S(1)}, bf16[64,1024]{1,0:T(8,128)(2,1)S(1)}, u32[]{:S(2)}, u32[]{:S(2)}) collective-permute-start(bf16[64,1024]{1,0:T(8,128)(2,1)S(1)} %slice.37), channel_id=1, source_target_pairs={{0,6},{1,7},{2,0},{3,1},{4,2},{5,3},{6,4},{7,5},{8,14},{9,15},{10,... | collective-permute-start | bytes 393224 | tf_op jit(solution)/shard_map/ppermute | solution.py:239
  43.8 12.7 %collective-permute-start.15 = (bf16[128,1024]{1,0:T(8,128)(2,1)S(1)}, bf16[128,1024]{1,0:T(8,128)(2,1)S(1)}, u32[]{:S(2)}, u32[]{:S(2)}) collective-permute-start(bf16[128,1024]{1,0:T(8,128)(2,1)S(1)} %collective-permute-done.11.refs_1_), channel_id=1, source_target_pairs={{0,6},{1,7},{2,0},{3,1},{4,2},{5,3},{6,4},{7,5},{8,14},{9,15},{10,... | collective-permute-start | bytes 786440 | tf_op jit(solution)/shard_map/ppermute | solution.py:241
  44.4 12.1 %collective-permute-start.14 = (bf16[128,1024]{1,0:T(8,128)(2,1)S(1)}, bf16[128,1024]{1,0:T(8,128)(2,1)S(1)}, u32[]{:S(2)}, u32[]{:S(2)}) collective-permute-start(bf16[128,1024]{1,0:T(8,128)(2,1)S(1)} %collective-permute-done.11.refs_1_), channel_id=1, source_target_pairs={{0,2},{1,3},{2,4},{3,5},{4,6},{5,7},{6,0},{7,1},{8,10},{9,11},{10,... | collective-permute-start | bytes 786440 | tf_op jit(solution)/shard_map/ppermute | solution.py:240
  47.3 15.0 %collective-permute-start.10 = (bf16[1024,256]{1,0:T(8,128)(2,1)S(1)}, bf16[1024,256]{1,0:T(8,128)(2,1)S(1)}, u32[]{:S(2)}, u32[]{:S(2)}) collective-permute-start(bf16[1024,256]{1,0:T(8,128)(2,1)S(1)} %pad_maximum_fusion.key_values), channel_id=1, source_target_pairs={{0,8},{8,0},{16,24},{24,16},{32,40},{40,32},{48,56},{56,48},{64,72... | collective-permute-start | bytes 1572872 | tf_op jit(solution)/shard_map/ppermute | solution.py:263
  48.4 8.1 %collective-permute-start.18 = (bf16[128,1024]{1,0:T(8,128)(2,1)S(1)}, bf16[128,1024]{1,0:T(8,128)(2,1)S(1)}, u32[]{:S(2)}, u32[]{:S(2)}) collective-permute-start(bf16[128,1024]{1,0:T(8,128)(2,1)S(1)} %constant_dynamic-update-slice_fusion.refs_6_), channel_id=1, source_target_pairs={{0,1},{1,0},{2,3},{3,2},{4,5},{5,4},{6,7},{7,6},{8,9},{9,8},{10,11... | collective-permute-start | bytes 786440 | tf_op jit(solution)/shard_map/ppermute | solution.py:243
  50.1 2.2 %copy-start = (bf16[32,256,256]{2,1,0:T(8,128)(2,1)S(1)}, bf16[32,256,256]{2,1,0:T(8,128)(2,1)}, u32[]{:S(2)}) copy-start(bf16[32,256,256]{2,1,0:T(8,128)(2,1)} %pages.1) | copy-start | bytes 12582916
  52.3 4.3 %copy-start.1 = (bf16[8192,128]{1,0:T(8,128)(2,1)S(1)}, bf16[8192,128]{1,0:T(8,128)(2,1)}, u32[]{:S(2)}) copy-start(bf16[8192,128]{1,0:T(8,128)(2,1)} %key_weight.1) | copy-start | bytes 6291460
  52.3 4.3 %copy-start.2 = (bf16[8192,128]{1,0:T(8,128)(2,1)S(1)}, bf16[8192,128]{1,0:T(8,128)(2,1)}, u32[]{:S(2)}) copy-start(bf16[8192,128]{1,0:T(8,128)(2,1)} %value_weight.1) | copy-start | bytes 6291460

commit v2 on v1

v2 whole, which is shorter than its diff:
```python
import math

import jax
import jax.numpy as jnp
from jax import lax
from jax.experimental import pallas as pl
from jax.experimental.pallas import tpu as pltpu
from jax.sharding import PartitionSpec as P

HEAD_SIZE = 128
CAP = 2
EPSILON = 1e-05
EXP_SCALE = math.log2(math.e) / math.sqrt(HEAD_SIZE)
VMEM_LIMIT = 16 * 1024 * 1024
BLOCK_ROWS = 128
Y, Z, CORE, X, PAIR = 4, 4, 2, 4, 2


def y_step(k):
    return [(i, (i + Z * CORE * k) % (Y * Z * CORE)) for i in range(Y * Z * CORE)]


def z_step(k):
    plane = Z * CORE
    return [(i, i // plane * plane + (i % plane + CORE * k) % plane) for i in range(Y * plane)]


def core_swap():
    return [(i, i ^ 1) for i in range(Y * Z * CORE)]


def x_step(k):
    return [(i, (i + PAIR * k) % (X * PAIR)) for i in range(X * PAIR)]


def pair_swap():
    return [(i, i ^ 1) for i in range(X * PAIR)]


def choose(index, options):
    chosen = options[0]
    for i in range(1, len(options)):
        chosen = jnp.where(index == i, options[i], chosen)
    return chosen


def together(*arrays):
    return lax.optimization_barrier(arrays)


def dot_nt(a, b):
    return lax.dot_general(a, b, (((1,), (1,)), ((), ())), preferred_element_type=jnp.float32)


def with_ones(key_values):
    ones = jnp.ones((key_values.shape[0], HEAD_SIZE), key_values.dtype)
    return jnp.concatenate([ones, key_values[:, HEAD_SIZE:]], axis=1)


def weighted(scores, highest, key_values):
    weights = jnp.exp2(scores * EXP_SCALE - highest * EXP_SCALE).astype(jnp.bfloat16)
    return jnp.dot(weights, with_ones(key_values), preferred_element_type=jnp.float32)


def page_kernel(lengths, queries, pages, sums, tops):
    count, span = pages.shape[:2]
    each = queries.shape[0] // count
    position = lax.broadcasted_iota(jnp.int32, (each, span), 1)
    for request in range(count):
        here = slice(request * each, (request + 1) * each)
        scores = dot_nt(queries[here, :], pages[request, :, :HEAD_SIZE])
        scores = jnp.where(position < lengths[request], scores, -jnp.inf)
        highest = jnp.max(scores, axis=1, keepdims=True)
        sums[here, :] = weighted(scores, highest, pages[request])
        tops[here, :] = highest


def page_part(lengths, queries, pages):
    count, span, width = pages.shape
    rows = queries.shape[0]
    vmem = pl.BlockSpec(memory_space=pltpu.VMEM)
    return pl.pallas_call(
        page_kernel,
        in_specs=[pl.BlockSpec(memory_space=pltpu.SMEM), vmem, vmem],
        out_specs=[vmem] * 2,
        out_shape=[
            jax.ShapeDtypeStruct((rows, 2 * HEAD_SIZE), jnp.float32),
            jax.ShapeDtypeStruct((rows, 1), jnp.float32),
        ],
        compiler_params=pltpu.CompilerParams(vmem_limit_bytes=VMEM_LIMIT),
        cost_estimate=pl.CostEstimate(
            flops=4 * rows * span * HEAD_SIZE, bytes_accessed=pages.size * 2, transcendentals=rows * span
        ),
    )(lengths, queries, pages)


def attend_rows(queries, key_values, sums, tops, here):
    scores = dot_nt(queries[here, :], key_values[:, :HEAD_SIZE])
    before = tops[here, :]
    highest = jnp.maximum(before, jnp.max(scores, axis=1, keepdims=True))
    total = sums[here, :] * jnp.exp2(before * EXP_SCALE - highest * EXP_SCALE)
    return total + weighted(scores, highest, key_values[...]), highest


def prefix_kernel(queries, key_values, sums, tops, new_sums, new_tops):
    for start in range(0, queries.shape[0], BLOCK_ROWS):
        here = slice(start, start + BLOCK_ROWS)
        new_sums[here, :], new_tops[here, :] = attend_rows(queries, key_values, sums, tops, here)


def prefix_part(queries, key_values, sums, tops):
    rows = queries.shape[0]
    span = key_values.shape[0]
    vmem = pl.BlockSpec(memory_space=pltpu.VMEM)
    return pl.pallas_call(
        prefix_kernel,
        in_specs=[vmem] * 4,
        out_specs=[vmem] * 2,
        out_shape=[
            jax.ShapeDtypeStruct(sums.shape, jnp.float32),
            jax.ShapeDtypeStruct(tops.shape, jnp.float32),
        ],
        compiler_params=pltpu.CompilerParams(vmem_limit_bytes=VMEM_LIMIT),
        cost_estimate=pl.CostEstimate(
            flops=8 * rows * span * HEAD_SIZE, bytes_accessed=span * 512, transcendentals=rows * span
        ),
    )(queries, key_values, sums, tops)


def project(owners, gain, key_weight, value_weight, blocks, out):
    tokens, wide = blocks[0].shape
    squares = jnp.zeros((tokens, 1), jnp.float32)
    for block in blocks:
        features = block[...].astype(jnp.float32)
        squares = squares + jnp.sum(features * features, axis=1, keepdims=True)
    scale = lax.rsqrt(squares / (wide * len(blocks)) + EPSILON)
    keys = jnp.zeros((tokens, HEAD_SIZE), jnp.float32)
    values = jnp.zeros((tokens, HEAD_SIZE), jnp.float32)
    for i, block in enumerate(blocks):
        rows = pl.ds(pl.multiple_of(owners[i] * wide, wide), wide)
        normed = block[...].astype(jnp.float32) * scale * gain[:, rows]
        normed = normed.astype(jnp.bfloat16)
        keys = keys + jnp.dot(normed, key_weight[rows, :], preferred_element_type=jnp.float32)
        values = values + jnp.dot(normed, value_weight[rows, :], preferred_element_type=jnp.float32)
    out[:, :HEAD_SIZE] = keys.astype(jnp.bfloat16)
    out[:, HEAD_SIZE:] = values.astype(jnp.bfloat16)


def finish_kernel(slots, owners, gain, key_weight, value_weight, queries, sums, tops, *refs):
    blocks, (out, recent) = refs[:-2], refs[-2:]
    out[...] = jnp.zeros_like(out)
    project(owners, gain, key_weight, value_weight, blocks, recent)
    each = out.shape[1]
    step_tokens = recent.shape[0] * each // queries.shape[0]
    heads = each // step_tokens
    for start in range(0, queries.shape[0], BLOCK_ROWS):
        here = slice(start, start + BLOCK_ROWS)
        scores = dot_nt(queries[here, :], recent[:, :HEAD_SIZE])
        row = lax.broadcasted_iota(jnp.int32, scores.shape, 0) + start
        token = lax.broadcasted_iota(jnp.int32, scores.shape, 1)
        seen = (row // each == token // step_tokens) & (
            token % step_tokens <= row % each // heads
        )
        scores = jnp.where(seen, scores, -jnp.inf)
        before = tops[here, :]
        highest = jnp.maximum(before, jnp.max(scores, axis=1, keepdims=True))
        total = sums[here, :] * jnp.exp2(before * EXP_SCALE - highest * EXP_SCALE)
        total = total + weighted(scores, highest, recent[...])
        result = (total[:, HEAD_SIZE:] / total[:, :HEAD_SIZE]).astype(jnp.bfloat16)
        for i in range(BLOCK_ROWS // each):
            out[slots[start // each + i]] = result[i * each : (i + 1) * each, :]


def finish(slots, owners, gain, key_weight, value_weight, queries, sums, tops, blocks, slot_count):
    rows = queries.shape[0]
    tokens = blocks[0].shape[0]
    vmem = pl.BlockSpec(memory_space=pltpu.VMEM)
    smem = pl.BlockSpec(memory_space=pltpu.SMEM)
    return pl.pallas_call(
        finish_kernel,
        in_specs=[smem, smem] + [vmem] * (6 + len(blocks)),
        out_specs=vmem,
        out_shape=jax.ShapeDtypeStruct((slot_count, rows // slots.shape[0], HEAD_SIZE), jnp.bfloat16),
        scratch_shapes=[pltpu.VMEM((tokens, 2 * HEAD_SIZE), jnp.bfloat16)],
        compiler_params=pltpu.CompilerParams(vmem_limit_bytes=VMEM_LIMIT),
        cost_estimate=pl.CostEstimate(
            flops=4 * tokens * key_weight.size, bytes_accessed=key_weight.size * 4, transcendentals=0
        ),
    )(slots, owners, gain.reshape(1, -1), key_weight, value_weight, queries, sums, tops, *blocks)


def per_device(
    prefix_kv,
    page_key_values,
    context_len,
    prefill_owner,
    assign,
    x_new,
    norm_gain,
    key_weight,
    value_weight,
    decoded_queries,
):
    row_count, step_count, width = decoded_queries.shape
    group_count = lax.axis_size("dp")
    assigned = assign[:, 0]
    indices = jnp.arange(row_count)
    matching = (assigned[:, None] == assigned[None, :]) & (indices[None, :] < indices[:, None])
    slots = assigned * CAP + jnp.sum(matching.astype(jnp.int32), axis=1)

    me, tensor = lax.axis_index("dp"), lax.axis_index("tensor")
    owner = prefill_owner[0]
    y, z, core = me // (Z * CORE), me // CORE % Z, me % CORE
    own_y, own_z, own_core = owner // (Z * CORE), owner // CORE % Z, owner % CORE
    x, pair = tensor // PAIR, tensor % PAIR
    half = prefix_kv.shape[0] // 2
    piece = half // Y
    queries = decoded_queries.reshape(-1, HEAD_SIZE)
    block = x_new.reshape(row_count * step_count, x_new.shape[2])

    other = lax.ppermute(prefix_kv, "dp", core_swap())
    twin = lax.ppermute(block, "tensor", pair_swap())
    left = lax.ppermute(block, "tensor", x_step(1))
    right = lax.ppermute(block, "tensor", x_step(X - 1))
    mine = jnp.where(core == own_core, prefix_kv[:half], other[half:])
    arrived = [mine[:piece]]
    for k in range(1, Y):
        arrived.append(lax.ppermute(mine[piece * k : piece * (k + 1)], "dp", y_step(k)))
    *arrived, twin = together(*arrived, twin)
    part = choose((y - own_y) % Y, arrived)

    page_sums, page_tops = page_part(context_len, queries, page_key_values)
    twin_left = lax.ppermute(twin, "tensor", x_step(1))
    twin_right = lax.ppermute(twin, "tensor", x_step(X - 1))
    far = lax.ppermute(jnp.concatenate([block, twin]), "tensor", x_step(2))
    arrived = [part] + [lax.ppermute(part, "dp", z_step(k)) for k in range(1, Z)]
    *arrived, left, right, twin_left, twin_right, page_sums = together(
        *arrived, left, right, twin_left, twin_right, page_sums
    )
    part = choose((z - own_z) % Z, arrived)

    places = [(0, 0), (0, 1), (X - 1, 0), (1, 0), (X - 1, 1), (1, 1), (2, 0), (2, 1)]
    owners = jnp.stack([(x + dx) % X * PAIR + (pair ^ flip) for dx, flip in places]).astype(jnp.int32)
    tokens = block.shape[0]
    blocks = [block, twin, left, right, twin_left, twin_right, far[:tokens], far[tokens:]]
    arrived = [part] + [lax.ppermute(part, "dp", y_step(k)) for k in range(1, Y)]
    near = jnp.concatenate(arrived)
    far_prefix = lax.ppermute(near, "dp", core_swap())
    sums, tops = prefix_part(queries, near, page_sums, page_tops)
    sums, tops = prefix_part(queries, far_prefix, sums, tops)
    slot_count = group_count * CAP
    result = finish(
        slots, owners, norm_gain, key_weight, value_weight, queries, sums, tops, blocks, slot_count
    )
    decoded = lax.all_to_all(
        result.reshape(group_count, CAP * 32, HEAD_SIZE), "dp", split_axis=0, concat_axis=0, tiled=True
    )
    return decoded.reshape(slot_count, step_count, width)


def solution(mesh):
    in_specs = (
        P("dp", "tensor"),
        P("dp", None, "tensor"),
        P("dp"),
        P(),
        P("dp", None),
        P("dp", None, "tensor"),
        P(),
        P(None, "tensor"),
        P(None, "tensor"),
        P("dp", None, "tensor"),
    )
    out_specs = P("dp", None, "tensor")
    return jax.shard_map(
        per_device, mesh=mesh, in_specs=in_specs, out_specs=out_specs, check_vma=False
    )
```

time: 95.3 us -> 87.8 us (0.921)
  Pallas kernels: 15.1 us -> 9.7 us
  waiting for transfers between devices: 15.5 us -> 11.6 us
  starting transfers between devices: 29.9 us -> 32.5 us
    pallas_call x4, Pallas kernels: 15.1 us -> 9.7 us  [the longest x2 3.81 us: prefix_part(): pl.pallas_call(prefix_kernel, in_specs=[vmem] * 4, out_specs=[vmem] * 2,...]
    ppermute x19 -> x17, waiting for transfers between devices: 15.5 us -> 11.6 us  [the longest x3 3.83 us: per_device(): lax.ppermute(part, 'dp', z_step(k))]
    ppermute x19 -> x17, starting transfers between devices: 29.9 us -> 32.5 us  [the longest x3 9.66 us: per_device(): lax.ppermute(part, 'dp', z_step(k))]
    slice x4 -> x2, local copies, waits for them, and re-layouts: 1.16 us -> 0.07 us  [the longest x1 0.04 us: per_device(): mine[piece * k:piece * (k + 1)]]
    unnamed x15 -> x14, local copies, waits for them, and re-layouts: 2.22 us -> 2.52 us
  transfers between devices with their start and end apart: 19 -> 17, of which waited for: 8 -> 6; matrix products, arithmetic and copies ran while one was open for 2% -> 3% of each run, Pallas kernels for 10% -> 5%
where the time goes in v2:
time: 87.8 us; the launch traced here: 87.6 us
  starting transfers between devices  32.5 us (37%)
  blocking collectives  26.8 us (31%)
  waiting for transfers between devices  11.6 us (13%)
  Pallas kernels  9.7 us (11%)
  local copies, waits for them, and re-layouts  4.71 us (5%)
  other arithmetic  1.43 us (2%)
    all_to_all x1, blocking collectives, per_device(): lax.all_to_all(result.reshape(group_count, CAP * 32, HEAD_SIZE), 'dp', sp...  26.8 us
    ppermute x3, starting transfers between devices, per_device(): lax.ppermute(part, 'dp', z_step(k))  9.66 us
    ppermute x3, starting transfers between devices, per_device(): lax.ppermute(part, 'dp', y_step(k))  4.72 us
    ppermute x3, starting transfers between devices, per_device(): lax.ppermute(mine[piece * k:piece * (k + 1)], 'dp', y_step(k))  4.27 us
    ppermute x3, waiting for transfers between devices, per_device(): lax.ppermute(part, 'dp', z_step(k))  3.83 us
    pallas_call x2, Pallas kernels, prefix_part(): pl.pallas_call(prefix_kernel, in_specs=[vmem] * 4, out_specs=[vmem] * 2,...  3.81 us
    pallas_call x1, Pallas kernels, finish(): pl.pallas_call(finish_kernel, in_specs=[smem, smem] + [vmem] * (6 + len(b...  3.67 us
    ppermute x1, starting transfers between devices, per_device(): far_prefix = lax.ppermute(near, 'dp', core_swap())  3.59 us
  transfers between devices with their start and end apart: 17, of which 6 were waited for; matrix products, arithmetic and copies ran while one was open for 3% of the time, Pallas kernels for 5%

profile of v2, /device:TPU:1, one launch (start us, length us, event | category | flops | bytes accessed | tf_op | source)
XLA Modules:
  0.0 87.6 jit_solution(5142966634375237707)
XLA Ops:
  0.0 0.0 copy-start.5
  0.0 3.2 %collective-permute-start = (bf16[2048,256]{1,0:T(8,128)(2,1)}, bf16[2048,256]{1,0:T(8,128)(2,1)S(1)}, u32[]{:S(2)}, u32[]{:S(2)}) collective-permute-start(bf16[2048,256]{1,0:T(8,128)(2,1)} %param.10), channel_id=1, source_target_pairs={{0,8},{8,0},{16,24},{24,16},{32,40},{40,32},{48,56},{56,48},{64,72... | collective-permute-start | bytes 3145736 | tf_op jit(solution)/shard_map/ppermute | solution.py:221
  3.2 1.0 %reshape.18.refs_0_ = bf16[128,1024]{1,0:T(8,128)(2,1)S(1)} reshape(bf16[32,4,1024]{2,1,0:T(4,128)(2,1)} %param.15) | data formatting | bytes 524288 | tf_op jit(solution)/shard_map/reshape | solution.py:219
  4.3 0.1 collective-permute-start.4
  5.0 0.0 copy-start.4
  5.1 0.7 collective-permute-done
  5.7 1.1 %slice_select_fusion = bf16[1024,256]{1,0:T(8,128)(2,1)S(1)} fusion(bf16[2048,256]{1,0:T(8,128)(2,1)S(1)} %collective-permute-done, bf16[2048,256]{1,0:T(8,128)(2,1)} %param.10, pred[]{:T(512)S(6)} %eq.55), kind=kLoop, calls=%fused_computation | loop fusion | flops 262144 | bytes 1572865 | tf_op jit(solution)/shard_map/jit(_where)/select_n | solution.py:225
  6.9 0.6 collective-permute-start.1
  7.5 2.6 %collective-permute-start.2 = (bf16[256,256]{1,0:T(8,128)(2,1)S(1)}, bf16[256,256]{1,0:T(8,128)(2,1)S(1)}, u32[]{:S(2)}, u32[]{:S(2)}) collective-permute-start(bf16[256,256]{1,0:T(8,128)(2,1)S(1)} %get-tuple-element.48), channel_id=1, source_target_pairs={{0,128},{8,136},{16,144},{24,152},{32,160},{40,168},{48,176},{56,1... | collective-permute-start | bytes 393224 | tf_op jit(solution)/shard_map/ppermute | solution.py:228
  10.1 1.1 %collective-permute-start.3 = (bf16[256,256]{1,0:T(8,128)(2,1)S(1)}, bf16[256,256]{1,0:T(8,128)(2,1)S(1)}, u32[]{:S(2)}, u32[]{:S(2)}) collective-permute-start(bf16[256,256]{1,0:T(8,128)(2,1)S(1)} %get-tuple-element.47), channel_id=1, source_target_pairs={{0,192},{8,200},{16,208},{24,216},{32,224},{40,232},{48,240},{56,2... | collective-permute-start | bytes 393224 | tf_op jit(solution)/shard_map/ppermute | solution.py:228
  11.2 1.2 %collective-permute-start.8 = (bf16[128,1024]{1,0:T(8,128)(2,1)S(1)}, bf16[128,1024]{1,0:T(8,128)(2,1)S(1)}, u32[]{:S(2)}, u32[]{:S(2)}) collective-permute-start(bf16[128,1024]{1,0:T(8,128)(2,1)S(1)} %reshape.18.refs_0_), channel_id=1, source_target_pairs={{0,2},{1,3},{2,4},{3,5},{4,6},{5,7},{6,0},{7,1},{8,10},{9,11},{10,... | collective-permute-start | bytes 786440 | tf_op jit(solution)/shard_map/ppermute | solution.py:223
  12.4 0.0 collective-permute-done.4.refs_1_
  12.4 1.5 %collective-permute-start.9 = (bf16[128,1024]{1,0:T(8,128)(2,1)S(1)}, bf16[128,1024]{1,0:T(8,128)(2,1)S(1)}, u32[]{:S(2)}, u32[]{:S(2)}) collective-permute-start(bf16[128,1024]{1,0:T(8,128)(2,1)S(1)} %reshape.18.refs_0_), channel_id=1, source_target_pairs={{0,6},{1,7},{2,0},{3,1},{4,2},{5,3},{6,4},{7,5},{8,14},{9,15},{10,... | collective-permute-start | bytes 786440 | tf_op jit(solution)/shard_map/ppermute | solution.py:224
  13.9 0.0 collective-permute-done.1
  13.9 2.3 %collective-permute-done.2 = bf16[256,256]{1,0:T(8,128)(2,1)S(1)} collective-permute-done((bf16[256,256]{1,0:T(8,128)(2,1)S(1)}, bf16[256,256]{1,0:T(8,128)(2,1)S(1)}, u32[]{:S(2)}, u32[]{:S(2)}) %collective-permute-start.2) | collective-permute-done | bytes 131104 | tf_op jit(solution)/shard_map/ppermute | solution.py:228
  16.2 0.0 collective-permute-done.3
  16.2 1.2 %collective-permute-start.10 = (bf16[128,1024]{1,0:T(8,128)(2,1)S(1)}, bf16[128,1024]{1,0:T(8,128)(2,1)S(1)}, u32[]{:S(2)}, u32[]{:S(2)}) collective-permute-start(bf16[128,1024]{1,0:T(8,128)(2,1)S(1)} %collective-permute-done.4.refs_1_), channel_id=1, source_target_pairs={{0,2},{1,3},{2,4},{3,5},{4,6},{5,7},{6,0},{7,1},{8,10},{9,11},{10,... | collective-permute-start | bytes 786440 | tf_op jit(solution)/shard_map/ppermute | solution.py:233
  17.4 1.5 %collective-permute-start.11 = (bf16[128,1024]{1,0:T(8,128)(2,1)S(1)}, bf16[128,1024]{1,0:T(8,128)(2,1)S(1)}, u32[]{:S(2)}, u32[]{:S(2)}) collective-permute-start(bf16[128,1024]{1,0:T(8,128)(2,1)S(1)} %collective-permute-done.4.refs_1_), channel_id=1, source_target_pairs={{0,6},{1,7},{2,0},{3,1},{4,2},{5,3},{6,4},{7,5},{8,14},{9,15},{10,... | collective-permute-start | bytes 786440 | tf_op jit(solution)/shard_map/ppermute | solution.py:234
  18.9 3.1 %collective-permute-start.5 = (bf16[256,256]{1,0:T(8,128)(2,1)S(1)}, bf16[256,256]{1,0:T(8,128)(2,1)S(1)}, u32[]{:S(2)}, u32[]{:S(2)}) collective-permute-start(bf16[256,256]{1,0:T(8,128)(2,1)S(1)} %select_select_fusion.1), channel_id=1, source_target_pairs={{0,16},{8,24},{16,32},{24,40},{32,48},{40,56},{48,0},{56,8},{64,80... | collective-permute-start | bytes 393224 | tf_op jit(solution)/shard_map/ppermute | solution.py:236
  22.0 0.0 collective-permute-done.8.refs_2_
  22.0 4.2 %collective-permute-start.6 = (bf16[256,256]{1,0:T(8,128)(2,1)S(1)}, bf16[256,256]{1,0:T(8,128)(2,1)S(1)}, u32[]{:S(2)}, u32[]{:S(2)}) collective-permute-start(bf16[256,256]{1,0:T(8,128)(2,1)S(1)} %select_select_fusion.1), channel_id=1, source_target_pairs={{0,32},{8,40},{16,48},{24,56},{32,0},{40,8},{48,16},{56,24},{64,96... | collective-permute-start | bytes 393224 | tf_op jit(solution)/shard_map/ppermute | solution.py:236
  26.2 0.0 collective-permute-done.9.refs_3_
  26.2 2.4 %collective-permute-start.7 = (bf16[256,256]{1,0:T(8,128)(2,1)S(1)}, bf16[256,256]{1,0:T(8,128)(2,1)S(1)}, u32[]{:S(2)}, u32[]{:S(2)}) collective-permute-start(bf16[256,256]{1,0:T(8,128)(2,1)S(1)} %select_select_fusion.1), channel_id=1, source_target_pairs={{0,48},{8,56},{16,0},{24,8},{32,16},{40,24},{48,32},{56,40},{64,11... | collective-permute-start | bytes 393224 | tf_op jit(solution)/shard_map/ppermute | solution.py:236
  28.6 0.0 copy-done.5
  28.6 0.1 reshape.17.queries
  28.7 0.1 stack.35.owners
  28.8 0.0 copy-done.4
  28.8 0.0 copy-start
  28.8 2.2 %copy-done = bf16[32,256,256]{2,1,0:T(8,128)(2,1)S(1)} copy-done((bf16[32,256,256]{2,1,0:T(8,128)(2,1)S(1)}, bf16[32,256,256]{2,1,0:T(8,128)(2,1)}, u32[]{:S(2)}) %copy-start) | copy-done | bytes 4194328
  31.0 0.0 copy-start.6
  31.0 2.2 %shard_map.100 = (f32[1024,256]{1,0:T(8,128)S(1)}, f32[1024,1]{1,0:T(8,128)S(1)}) custom-call(s32[32]{0:T(128)S(1)} %copy-done.4, bf16[1024,128]{1,0:T(8,128)(2,1)S(1)} %reshape.17.queries, bf16[32,256,256]{2,1,0:T(8,128)(2,1)S(1)} %copy-done), custom_call_target="tpu_custom_call" | custom-call | flops 134217728 | bytes 4194304 | tf_op jit(solution)/shard_map/pallas_call | solution.py:82
  33.2 0.0 collective-permute-done.5
  33.2 0.1 collective-permute-done.6
  33.3 3.7 %collective-permute-done.7 = bf16[256,256]{1,0:T(8,128)(2,1)S(1)} collective-permute-done((bf16[256,256]{1,0:T(8,128)(2,1)S(1)}, bf16[256,256]{1,0:T(8,128)(2,1)S(1)}, u32[]{:S(2)}, u32[]{:S(2)}) %collective-permute-start.7) | collective-permute-done | bytes 131104 | tf_op jit(solution)/shard_map/ppermute | solution.py:236
  37.0 0.0 collective-permute-done.10.refs_4_
  37.0 0.0 collective-permute-done.11.refs_5_
  37.1 2.2 %collective-permute-start.12 = (bf16[256,256]{1,0:T(8,128)(2,1)S(1)}, bf16[256,256]{1,0:T(8,128)(2,1)S(1)}, u32[]{:S(2)}, u32[]{:S(2)}) collective-permute-start(bf16[256,256]{1,0:T(8,128)(2,1)S(1)} %select_select_fusion), channel_id=1, source_target_pairs={{0,64},{8,72},{16,80},{24,88},{32,96},{40,104},{48,112},{56,120},{... | collective-permute-start | bytes 393224 | tf_op jit(solution)/shard_map/ppermute | solution.py:246
  39.3 1.0 %collective-permute-start.13 = (bf16[256,256]{1,0:T(8,128)(2,1)S(1)}, bf16[256,256]{1,0:T(8,128)(2,1)S(1)}, u32[]{:S(2)}, u32[]{:S(2)}) collective-permute-start(bf16[256,256]{1,0:T(8,128)(2,1)S(1)} %select_select_fusion), channel_id=1, source_target_pairs={{0,128},{8,136},{16,144},{24,152},{32,160},{40,168},{48,176},{56,1... | collective-permute-start | bytes 393224 | tf_op jit(solution)/shard_map/ppermute | solution.py:246
  40.3 1.5 %collective-permute-start.14 = (bf16[256,256]{1,0:T(8,128)(2,1)S(1)}, bf16[256,256]{1,0:T(8,128)(2,1)S(1)}, u32[]{:S(2)}, u32[]{:S(2)}) collective-permute-start(bf16[256,256]{1,0:T(8,128)(2,1)S(1)} %select_select_fusion), channel_id=1, source_target_pairs={{0,192},{8,200},{16,208},{24,216},{32,224},{40,232},{48,240},{56,2... | collective-permute-start | bytes 393224 | tf_op jit(solution)/shard_map/ppermute | solution.py:246
  41.8 1.6 %collective-permute-start.16 = (bf16[256,1024]{1,0:T(8,128)(2,1)S(1)}, bf16[256,1024]{1,0:T(8,128)(2,1)S(1)}, u32[]{:S(2)}, u32[]{:S(2)}) collective-permute-start(bf16[256,1024]{1,0:T(8,128)(2,1)S(1)} %pad_maximum_fusion.1), channel_id=1, source_target_pairs={{0,4},{1,5},{2,6},{3,7},{4,0},{5,1},{6,2},{7,3},{8,12},{9,13},{10,... | collective-permute-start | bytes 1572872 | tf_op jit(solution)/shard_map/ppermute | solution.py:235
  43.5 0.0 copy-done.6
  43.5 0.2 convert_reduce_fusion
  43.6 0.0 collective-permute-done.12
  43.6 1.3 %collective-permute-done.13 = bf16[256,256]{1,0:T(8,128)(2,1)S(1)} collective-permute-done((bf16[256,256]{1,0:T(8,128)(2,1)S(1)}, bf16[256,256]{1,0:T(8,128)(2,1)S(1)}, u32[]{:S(2)}, u32[]{:S(2)}) %collective-permute-start.13) | collective-permute-done | bytes 131104 | tf_op jit(solution)/shard_map/ppermute | solution.py:246
  44.9 0.0 collective-permute-done.14
  45.0 3.6 %collective-permute-start.15 = (bf16[1024,256]{1,0:T(8,128)(2,1)S(1)}, bf16[1024,256]{1,0:T(8,128)(2,1)S(1)}, u32[]{:S(2)}, u32[]{:S(2)}) collective-permute-start(bf16[1024,256]{1,0:T(8,128)(2,1)S(1)} %pad_maximum_fusion.key_values), channel_id=1, source_target_pairs={{0,8},{8,0},{16,24},{24,16},{32,40},{40,32},{48,56},{56,48},{64,72... | collective-permute-start | bytes 1572872 | tf_op jit(solution)/shard_map/ppermute | solution.py:248
  48.6 2.0 %shard_map.101 = (f32[1024,256]{1,0:T(8,128)S(1)}, f32[1024,1]{1,0:T(8,128)S(1)}) custom-call(bf16[1024,128]{1,0:T(8,128)(2,1)S(1)} %reshape.17.queries, bf16[1024,256]{1,0:T(8,128)(2,1)S(1)} %pad_maximum_fusion.key_values, f32[1024,256]{1,0:T(8,128)S(1)} %get-tuple-element.35.sums, f32[1024,1]{1,0:T(8,128)S(1)} %get-tuple-element.36.tops), custom_call_target="tpu_custom_call" | custom-call | flops 1073741824 | bytes 524288 | tf_op jit(solution)/shard_map/pallas_call | solution.py:115
  50.5 3.4 %collective-permute-done.16 = bf16[256,1024]{1,0:T(8,128)(2,1)S(1)} collective-permute-done((bf16[256,1024]{1,0:T(8,128)(2,1)S(1)}, bf16[256,1024]{1,0:T(8,128)(2,1)S(1)}, u32[]{:S(2)}, u32[]{:S(2)}) %collective-permute-start.16) | collective-permute-done | bytes 524320 | tf_op jit(solution)/shard_map/ppermute | solution.py:235
  54.0 0.0 copy-start.2
  54.0 0.0 copy-start.1
  54.0 0.0 copy-start.3
  54.0 0.0 collective-permute-done.15.key_values
  54.0 1.8 %shard_map.102 = (f32[1024,256]{1,0:T(8,128)S(1)}, f32[1024,1]{1,0:T(8,128)S(1)}) custom-call(bf16[1024,128]{1,0:T(8,128)(2,1)S(1)} %reshape.17.queries, bf16[1024,256]{1,0:T(8,128)(2,1)S(1)} %collective-permute-done.15.key_values, f32[1024,256]{1,0:T(8,128)S(1)} %get-tuple-element.37.sums, f32[1024,1]{1,0:T(8,128)S(1)} %get-tuple-element.38.tops), custom_call_target="tpu_custom_call" | custom-call | flops 1073741824 | bytes 524288 | tf_op jit(solution)/shard_map/pallas_call | solution.py:115
  55.9 0.0 copy-done.2
  55.9 0.3 copy-done.1
  56.2 0.0 copy-done.3
  56.2 3.7 %shard_map.103 = bf16[64,32,128]{2,1,0:T(8,128)(2,1)S(1)} custom-call(s32[32]{0:T(128)S(1)} %multiply_add_fusion.slots, s32[8]{0:T(128)S(1)} %stack.35.owners, f32[1,8192]{1,0:T(1,128)S(1)} %bitcast.18, bf16[8192,128]{1,0:T(8,128)(2,1)S(1)} %copy-done.1, bf16[8192,128]{1,0:T(8,128)(2,1)S(1)} %copy-done.2, bf16[1024,128]{1,0:T(8,128)(2,1)S(1)} %reshape.17.queries, ...), custom_call_target="tpu_custom_call" | custom-call | flops 536870912 | bytes 4194304 | tf_op jit(solution)/shard_map/pallas_call | solution.py:179
  59.9 26.8 %all_to_all.5 = bf16[32,64,128]{2,1,0:T(8,128)(2,1)S(1)} all-to-all(bf16[32,64,128]{2,1,0:T(8,128)(2,1)S(1)} %bitcast.17), channel_id=1, replica_groups=mesh['dp'=32,'tensor'=8] {'dp'}, dimensions={0} | all-to-all | bytes 1048576 | tf_op jit(solution)/shard_map/all_to_all | solution.py:255
  86.7 0.9 %reshape.20 = bf16[64,4,1024]{2,1,0:T(4,128)(2,1)} reshape(bf16[32,64,128]{2,1,0:T(8,128)(2,1)S(1)} %all_to_all.5) | data formatting | bytes 1048576 | tf_op jit(solution)/shard_map/reshape | solution.py:258
  (7 shorter events, 0.2 us)
Async XLA Ops:
  0.0 28.6 %copy-start.5 = (bf16[32,4,1024]{2,1,0:T(4,128)(2,1)S(1)}, bf16[32,4,1024]{2,1,0:T(4,128)(2,1)}, u32[]{:S(2)}) copy-start(bf16[32,4,1024]{2,1,0:T(4,128)(2,1)} %param.19) | copy-start | bytes 786436
  0.0 5.7 %collective-permute-start = (bf16[2048,256]{1,0:T(8,128)(2,1)}, bf16[2048,256]{1,0:T(8,128)(2,1)S(1)}, u32[]{:S(2)}, u32[]{:S(2)}) collective-permute-start(bf16[2048,256]{1,0:T(8,128)(2,1)} %param.10), channel_id=1, source_target_pairs={{0,8},{8,0},{16,24},{24,16},{32,40},{40,32},{48,56},{56,48},{64,72... | collective-permute-start | bytes 3145736 | tf_op jit(solution)/shard_map/ppermute | solution.py:221
  4.3 8.1 %collective-permute-start.4 = (bf16[128,1024]{1,0:T(8,128)(2,1)S(1)}, bf16[128,1024]{1,0:T(8,128)(2,1)S(1)}, u32[]{:S(2)}, u32[]{:S(2)}) collective-permute-start(bf16[128,1024]{1,0:T(8,128)(2,1)S(1)} %reshape.18.refs_0_), channel_id=1, source_target_pairs={{0,1},{1,0},{2,3},{3,2},{4,5},{5,4},{6,7},{7,6},{8,9},{9,8},{10,11... | collective-permute-start | bytes 786440 | tf_op jit(solution)/shard_map/ppermute | solution.py:222
  5.0 23.8 %copy-start.4 = (s32[32]{0:T(128)S(1)}, s32[32]{0:T(128)}, u32[]{:S(2)}) copy-start(s32[32]{0:T(128)} %lengths.1) | copy-start | bytes 388
  6.9 7.0 %collective-permute-start.1 = (bf16[256,256]{1,0:T(8,128)(2,1)S(1)}, bf16[256,256]{1,0:T(8,128)(2,1)S(1)}, u32[]{:S(2)}, u32[]{:S(2)}) collective-permute-start(bf16[256,256]{1,0:T(8,128)(2,1)S(1)} %get-tuple-element.49), channel_id=1, source_target_pairs={{0,64},{8,72},{16,80},{24,88},{32,96},{40,104},{48,112},{56,120},{... | collective-permute-start | bytes 393224 | tf_op jit(solution)/shard_map/ppermute | solution.py:228
  7.5 8.7 %collective-permute-start.2 = (bf16[256,256]{1,0:T(8,128)(2,1)S(1)}, bf16[256,256]{1,0:T(8,128)(2,1)S(1)}, u32[]{:S(2)}, u32[]{:S(2)}) collective-permute-start(bf16[256,256]{1,0:T(8,128)(2,1)S(1)} %get-tuple-element.48), channel_id=1, source_target_pairs={{0,128},{8,136},{16,144},{24,152},{32,160},{40,168},{48,176},{56,1... | collective-permute-start | bytes 393224 | tf_op jit(solution)/shard_map/ppermute | solution.py:228
  10.1 6.1 %collective-permute-start.3 = (bf16[256,256]{1,0:T(8,128)(2,1)S(1)}, bf16[256,256]{1,0:T(8,128)(2,1)S(1)}, u32[]{:S(2)}, u32[]{:S(2)}) collective-permute-start(bf16[256,256]{1,0:T(8,128)(2,1)S(1)} %get-tuple-element.47), channel_id=1, source_target_pairs={{0,192},{8,200},{16,208},{24,216},{32,224},{40,232},{48,240},{56,2... | collective-permute-start | bytes 393224 | tf_op jit(solution)/shard_map/ppermute | solution.py:228
  11.2 10.8 %collective-permute-start.8 = (bf16[128,1024]{1,0:T(8,128)(2,1)S(1)}, bf16[128,1024]{1,0:T(8,128)(2,1)S(1)}, u32[]{:S(2)}, u32[]{:S(2)}) collective-permute-start(bf16[128,1024]{1,0:T(8,128)(2,1)S(1)} %reshape.18.refs_0_), channel_id=1, source_target_pairs={{0,2},{1,3},{2,4},{3,5},{4,6},{5,7},{6,0},{7,1},{8,10},{9,11},{10,... | collective-permute-start | bytes 786440 | tf_op jit(solution)/shard_map/ppermute | solution.py:223
  12.4 13.8 %collective-permute-start.9 = (bf16[128,1024]{1,0:T(8,128)(2,1)S(1)}, bf16[128,1024]{1,0:T(8,128)(2,1)S(1)}, u32[]{:S(2)}, u32[]{:S(2)}) collective-permute-start(bf16[128,1024]{1,0:T(8,128)(2,1)S(1)} %reshape.18.refs_0_), channel_id=1, source_target_pairs={{0,6},{1,7},{2,0},{3,1},{4,2},{5,3},{6,4},{7,5},{8,14},{9,15},{10,... | collective-permute-start | bytes 786440 | tf_op jit(solution)/shard_map/ppermute | solution.py:224
  16.2 20.8 %collective-permute-start.10 = (bf16[128,1024]{1,0:T(8,128)(2,1)S(1)}, bf16[128,1024]{1,0:T(8,128)(2,1)S(1)}, u32[]{:S(2)}, u32[]{:S(2)}) collective-permute-start(bf16[128,1024]{1,0:T(8,128)(2,1)S(1)} %collective-permute-done.4.refs_1_), channel_id=1, source_target_pairs={{0,2},{1,3},{2,4},{3,5},{4,6},{5,7},{6,0},{7,1},{8,10},{9,11},{10,... | collective-permute-start | bytes 786440 | tf_op jit(solution)/shard_map/ppermute | solution.py:233
  17.4 19.6 %collective-permute-start.11 = (bf16[128,1024]{1,0:T(8,128)(2,1)S(1)}, bf16[128,1024]{1,0:T(8,128)(2,1)S(1)}, u32[]{:S(2)}, u32[]{:S(2)}) collective-permute-start(bf16[128,1024]{1,0:T(8,128)(2,1)S(1)} %collective-permute-done.4.refs_1_), channel_id=1, source_target_pairs={{0,6},{1,7},{2,0},{3,1},{4,2},{5,3},{6,4},{7,5},{8,14},{9,15},{10,... | collective-permute-start | bytes 786440 | tf_op jit(solution)/shard_map/ppermute | solution.py:234
  18.9 14.3 %collective-permute-start.5 = (bf16[256,256]{1,0:T(8,128)(2,1)S(1)}, bf16[256,256]{1,0:T(8,128)(2,1)S(1)}, u32[]{:S(2)}, u32[]{:S(2)}) collective-permute-start(bf16[256,256]{1,0:T(8,128)(2,1)S(1)} %select_select_fusion.1), channel_id=1, source_target_pairs={{0,16},{8,24},{16,32},{24,40},{32,48},{40,56},{48,0},{56,8},{64,80... | collective-permute-start | bytes 393224 | tf_op jit(solution)/shard_map/ppermute | solution.py:236
  22.0 11.3 %collective-permute-start.6 = (bf16[256,256]{1,0:T(8,128)(2,1)S(1)}, bf16[256,256]{1,0:T(8,128)(2,1)S(1)}, u32[]{:S(2)}, u32[]{:S(2)}) collective-permute-start(bf16[256,256]{1,0:T(8,128)(2,1)S(1)} %select_select_fusion.1), channel_id=1, source_target_pairs={{0,32},{8,40},{16,48},{24,56},{32,0},{40,8},{48,16},{56,24},{64,96... | collective-permute-start | bytes 393224 | tf_op jit(solution)/shard_map/ppermute | solution.py:236
  26.2 10.8 %collective-permute-start.7 = (bf16[256,256]{1,0:T(8,128)(2,1)S(1)}, bf16[256,256]{1,0:T(8,128)(2,1)S(1)}, u32[]{:S(2)}, u32[]{:S(2)}) collective-permute-start(bf16[256,256]{1,0:T(8,128)(2,1)S(1)} %select_select_fusion.1), channel_id=1, source_target_pairs={{0,48},{8,56},{16,0},{24,8},{32,16},{40,24},{48,32},{56,40},{64,11... | collective-permute-start | bytes 393224 | tf_op jit(solution)/shard_map/ppermute | solution.py:236
  28.8 2.2 %copy-start = (bf16[32,256,256]{2,1,0:T(8,128)(2,1)S(1)}, bf16[32,256,256]{2,1,0:T(8,128)(2,1)}, u32[]{:S(2)}) copy-start(bf16[32,256,256]{2,1,0:T(8,128)(2,1)} %pages.1) | copy-start | bytes 12582916
  31.0 12.5 %copy-start.6 = (s32[32,1]{0,1:T(1,128)S(1)}, s32[32,1]{0,1:T(1,128)}, u32[]{:S(2)}) copy-start(s32[32,1]{0,1:T(1,128)} %param.14) | copy-start | bytes 388
  37.1 6.6 %collective-permute-start.12 = (bf16[256,256]{1,0:T(8,128)(2,1)S(1)}, bf16[256,256]{1,0:T(8,128)(2,1)S(1)}, u32[]{:S(2)}, u32[]{:S(2)}) collective-permute-start(bf16[256,256]{1,0:T(8,128)(2,1)S(1)} %select_select_fusion), channel_id=1, source_target_pairs={{0,64},{8,72},{16,80},{24,88},{32,96},{40,104},{48,112},{56,120},{... | collective-permute-start | bytes 393224 | tf_op jit(solution)/shard_map/ppermute | solution.py:246
  39.3 5.6 %collective-permute-start.13 = (bf16[256,256]{1,0:T(8,128)(2,1)S(1)}, bf16[256,256]{1,0:T(8,128)(2,1)S(1)}, u32[]{:S(2)}, u32[]{:S(2)}) collective-permute-start(bf16[256,256]{1,0:T(8,128)(2,1)S(1)} %select_select_fusion), channel_id=1, source_target_pairs={{0,128},{8,136},{16,144},{24,152},{32,160},{40,168},{48,176},{56,1... | collective-permute-start | bytes 393224 | tf_op jit(solution)/shard_map/ppermute | solution.py:246
  40.3 4.6 %collective-permute-start.14 = (bf16[256,256]{1,0:T(8,128)(2,1)S(1)}, bf16[256,256]{1,0:T(8,128)(2,1)S(1)}, u32[]{:S(2)}, u32[]{:S(2)}) collective-permute-start(bf16[256,256]{1,0:T(8,128)(2,1)S(1)} %select_select_fusion), channel_id=1, source_target_pairs={{0,192},{8,200},{16,208},{24,216},{32,224},{40,232},{48,240},{56,2... | collective-permute-start | bytes 393224 | tf_op jit(solution)/shard_map/ppermute | solution.py:246
  41.8 12.1 %collective-permute-start.16 = (bf16[256,1024]{1,0:T(8,128)(2,1)S(1)}, bf16[256,1024]{1,0:T(8,128)(2,1)S(1)}, u32[]{:S(2)}, u32[]{:S(2)}) collective-permute-start(bf16[256,1024]{1,0:T(8,128)(2,1)S(1)} %pad_maximum_fusion.1), channel_id=1, source_target_pairs={{0,4},{1,5},{2,6},{3,7},{4,0},{5,1},{6,2},{7,3},{8,12},{9,13},{10,... | collective-permute-start | bytes 1572872 | tf_op jit(solution)/shard_map/ppermute | solution.py:235
  45.0 9.1 %collective-permute-start.15 = (bf16[1024,256]{1,0:T(8,128)(2,1)S(1)}, bf16[1024,256]{1,0:T(8,128)(2,1)S(1)}, u32[]{:S(2)}, u32[]{:S(2)}) collective-permute-start(bf16[1024,256]{1,0:T(8,128)(2,1)S(1)} %pad_maximum_fusion.key_values), channel_id=1, source_target_pairs={{0,8},{8,0},{16,24},{24,16},{32,40},{40,32},{48,56},{56,48},{64,72... | collective-permute-start | bytes 1572872 | tf_op jit(solution)/shard_map/ppermute | solution.py:248
  54.0 1.9 %copy-start.2 = (bf16[8192,128]{1,0:T(8,128)(2,1)S(1)}, bf16[8192,128]{1,0:T(8,128)(2,1)}, u32[]{:S(2)}) copy-start(bf16[8192,128]{1,0:T(8,128)(2,1)} %value_weight.1) | copy-start | bytes 6291460
  54.0 2.2 %copy-start.1 = (bf16[8192,128]{1,0:T(8,128)(2,1)S(1)}, bf16[8192,128]{1,0:T(8,128)(2,1)}, u32[]{:S(2)}) copy-start(bf16[8192,128]{1,0:T(8,128)(2,1)} %key_weight.1) | copy-start | bytes 6291460
  54.0 2.2 %copy-start.3 = (f32[8192]{0:T(1024)S(1)}, f32[8192]{0:T(1024)}, u32[]{:S(2)}) copy-start(f32[8192]{0:T(1024)} %param.16) | copy-start | bytes 98308

commit v3 on v2

--- a/solution.py
+++ b/solution.py
@@ -147,7 +147,9 @@
 
 
 def finish_kernel(slots, owners, gain, key_weight, value_weight, queries, sums, tops, *refs):
-    blocks, (out, recent) = refs[:-2], refs[-2:]
+    (*blocks, far), (out, recent) = refs[:-2], refs[-2:]
+    tokens = recent.shape[0]
+    blocks = [*blocks, far.at[:tokens], far.at[tokens:]]
     out[...] = jnp.zeros_like(out)
     project(owners, gain, key_weight, value_weight, blocks, recent)
     each = out.shape[1]
@@ -234,16 +236,14 @@
     twin_right = lax.ppermute(twin, "tensor", x_step(X - 1))
     far = lax.ppermute(jnp.concatenate([block, twin]), "tensor", x_step(2))
     arrived = [part] + [lax.ppermute(part, "dp", z_step(k)) for k in range(1, Z)]
-    *arrived, left, right, twin_left, twin_right, page_sums = together(
-        *arrived, left, right, twin_left, twin_right, page_sums
-    )
+    *arrived, left, right, page_sums = together(*arrived, left, right, page_sums)
     part = choose((z - own_z) % Z, arrived)
 
     places = [(0, 0), (0, 1), (X - 1, 0), (1, 0), (X - 1, 1), (1, 1), (2, 0), (2, 1)]
     owners = jnp.stack([(x + dx) % X * PAIR + (pair ^ flip) for dx, flip in places]).astype(jnp.int32)
-    tokens = block.shape[0]
-    blocks = [block, twin, left, right, twin_left, twin_right, far[:tokens], far[tokens:]]
     arrived = [part] + [lax.ppermute(part, "dp", y_step(k)) for k in range(1, Y)]
+    arrived[1], twin_left, twin_right, far = together(arrived[1], twin_left, twin_right, far)
+    blocks = [block, twin, left, right, twin_left, twin_right, far]
     near = jnp.concatenate(arrived)
     far_prefix = lax.ppermute(near, "dp", core_swap())
     sums, tops = prefix_part(queries, near, page_sums, page_tops)

time: 87.8 us -> 86.2 us (0.982)
  blocking collectives: 26.8 us -> 23 us
  waiting for transfers between devices: 11.6 us -> 9.68 us
  local copies, waits for them, and re-layouts: 4.71 us -> 6.61 us
  Pallas kernels: 9.7 us -> 10.6 us
    all_to_all x1, blocking collectives: 26.8 us -> 23 us  [per_device(): lax.all_to_all(result.reshape(group_count, CAP * 32, HEAD_SIZE), 'dp', sp...]
    ppermute x3, waiting for transfers between devices: 3.83 us -> 0.01 us  [per_device(): lax.ppermute(part, 'dp', z_step(k))]
    ppermute x1, waiting for transfers between devices: 3.44 us -> 0.01 us  [per_device(): far = lax.ppermute(jnp.concatenate([block, twin]), 'tensor', x_step(2))]
    ppermute x1, waiting for transfers between devices: 0.01 us -> 3.12 us  [per_device(): twin_left = lax.ppermute(twin, 'tensor', x_step(1))]
    ppermute x3, waiting for transfers between devices: 1.29 us -> 3.44 us  [per_device(): lax.ppermute(part, 'dp', y_step(k))]
    unnamed x14 -> x18, local copies, waits for them, and re-layouts: 2.52 us -> 4.46 us
    ppermute x1, starting transfers between devices: 1.62 us -> 2.74 us  [per_device(): far = lax.ppermute(jnp.concatenate([block, twin]), 'tensor', x_step(2))]
    pallas_call x2, Pallas kernels: 3.81 us -> 4.74 us  [prefix_part(): pl.pallas_call(prefix_kernel, in_specs=[vmem] * 4, out_specs=[vmem] * 2,...]
  transfers between devices with their start and end apart: 17 -> 17, of which waited for: 6 -> 5; matrix products, arithmetic and copies ran while one was open for 3% -> 4% of each run, Pallas kernels for 5% -> 5%
where the time goes in v3:
time: 86.2 us; the launch traced here: 85.9 us
  starting transfers between devices  32.9 us (38%)
  blocking collectives  23 us (27%)
  Pallas kernels  10.6 us (12%)
  waiting for transfers between devices  9.68 us (11%)
  local copies, waits for them, and re-layouts  6.61 us (8%)
  other arithmetic  2.21 us (3%)
    all_to_all x1, blocking collectives, per_device(): lax.all_to_all(result.reshape(group_count, CAP * 32, HEAD_SIZE), 'dp', sp...  23 us
    ppermute x3, starting transfers between devices, per_device(): lax.ppermute(part, 'dp', z_step(k))  9.62 us
    pallas_call x2, Pallas kernels, prefix_part(): pl.pallas_call(prefix_kernel, in_specs=[vmem] * 4, out_specs=[vmem] * 2,...  4.74 us
    unnamed x18, local copies, waits for them, and re-layouts  4.46 us
    ppermute x3, starting transfers between devices, per_device(): lax.ppermute(mine[piece * k:piece * (k + 1)], 'dp', y_step(k))  4.31 us
    ppermute x3, starting transfers between devices, per_device(): lax.ppermute(part, 'dp', y_step(k))  4.01 us
    pallas_call x1, Pallas kernels, finish(): pl.pallas_call(finish_kernel, in_specs=[smem, smem] + [vmem] * (6 + len(b...  3.68 us
    ppermute x1, starting transfers between devices, per_device(): far_prefix = lax.ppermute(near, 'dp', core_swap())  3.56 us
  transfers between devices with their start and end apart: 17, of which 5 were waited for; matrix products, arithmetic and copies ran while one was open for 4% of the time, Pallas kernels for 5%

profile of v3, /device:TPU:1, one launch (start us, length us, event | category | flops | bytes accessed | tf_op | source)
XLA Modules:
  0.0 85.9 jit_solution(3892616412286227153)
XLA Ops:
  0.0 3.2 %collective-permute-start = (bf16[2048,256]{1,0:T(8,128)(2,1)}, bf16[2048,256]{1,0:T(8,128)(2,1)S(1)}, u32[]{:S(2)}, u32[]{:S(2)}) collective-permute-start(bf16[2048,256]{1,0:T(8,128)(2,1)} %param.10), channel_id=1, source_target_pairs={{0,8},{8,0},{16,24},{24,16},{32,40},{40,32},{48,56},{56,48},{64,72... | collective-permute-start | bytes 3145736 | tf_op jit(solution)/shard_map/ppermute | solution.py:223
  3.2 1.0 %reshape.18.refs_0_ = bf16[128,1024]{1,0:T(8,128)(2,1)S(1)} reshape(bf16[32,4,1024]{2,1,0:T(4,128)(2,1)} %param.15) | data formatting | bytes 524288 | tf_op jit(solution)/shard_map/reshape | solution.py:221
  4.3 0.1 collective-permute-start.4
  5.0 0.0 copy-start.7
  5.1 0.7 collective-permute-done
  5.7 1.1 %slice_select_fusion = bf16[1024,256]{1,0:T(8,128)(2,1)S(1)} fusion(bf16[2048,256]{1,0:T(8,128)(2,1)S(1)} %collective-permute-done, bf16[2048,256]{1,0:T(8,128)(2,1)} %param.10, pred[]{:T(512)S(6)} %eq.55), kind=kLoop, calls=%fused_computation | loop fusion | flops 262144 | bytes 1572865 | tf_op jit(solution)/shard_map/jit(_where)/select_n | solution.py:227
  6.8 0.0 copy-start.4
  6.9 0.6 collective-permute-start.1
  7.5 2.6 %collective-permute-start.2 = (bf16[256,256]{1,0:T(8,128)(2,1)S(1)}, bf16[256,256]{1,0:T(8,128)(2,1)S(1)}, u32[]{:S(2)}, u32[]{:S(2)}) collective-permute-start(bf16[256,256]{1,0:T(8,128)(2,1)S(1)} %get-tuple-element.50), channel_id=1, source_target_pairs={{0,128},{8,136},{16,144},{24,152},{32,160},{40,168},{48,176},{56,1... | collective-permute-start | bytes 393224 | tf_op jit(solution)/shard_map/ppermute | solution.py:230
  10.1 1.1 %collective-permute-start.3 = (bf16[256,256]{1,0:T(8,128)(2,1)S(1)}, bf16[256,256]{1,0:T(8,128)(2,1)S(1)}, u32[]{:S(2)}, u32[]{:S(2)}) collective-permute-start(bf16[256,256]{1,0:T(8,128)(2,1)S(1)} %get-tuple-element.49), channel_id=1, source_target_pairs={{0,192},{8,200},{16,208},{24,216},{32,224},{40,232},{48,240},{56,2... | collective-permute-start | bytes 393224 | tf_op jit(solution)/shard_map/ppermute | solution.py:230
  11.2 1.2 %collective-permute-start.8 = (bf16[128,1024]{1,0:T(8,128)(2,1)S(1)}, bf16[128,1024]{1,0:T(8,128)(2,1)S(1)}, u32[]{:S(2)}, u32[]{:S(2)}) collective-permute-start(bf16[128,1024]{1,0:T(8,128)(2,1)S(1)} %reshape.18.refs_0_), channel_id=1, source_target_pairs={{0,2},{1,3},{2,4},{3,5},{4,6},{5,7},{6,0},{7,1},{8,10},{9,11},{10,... | collective-permute-start | bytes 786440 | tf_op jit(solution)/shard_map/ppermute | solution.py:225
  12.4 0.0 collective-permute-done.4.refs_1_
  12.4 1.5 %collective-permute-start.9 = (bf16[128,1024]{1,0:T(8,128)(2,1)S(1)}, bf16[128,1024]{1,0:T(8,128)(2,1)S(1)}, u32[]{:S(2)}, u32[]{:S(2)}) collective-permute-start(bf16[128,1024]{1,0:T(8,128)(2,1)S(1)} %reshape.18.refs_0_), channel_id=1, source_target_pairs={{0,6},{1,7},{2,0},{3,1},{4,2},{5,3},{6,4},{7,5},{8,14},{9,15},{10,... | collective-permute-start | bytes 786440 | tf_op jit(solution)/shard_map/ppermute | solution.py:226
  13.9 0.0 collective-permute-done.1
  13.9 2.4 %collective-permute-done.2 = bf16[256,256]{1,0:T(8,128)(2,1)S(1)} collective-permute-done((bf16[256,256]{1,0:T(8,128)(2,1)S(1)}, bf16[256,256]{1,0:T(8,128)(2,1)S(1)}, u32[]{:S(2)}, u32[]{:S(2)}) %collective-permute-start.2) | collective-permute-done | bytes 131104 | tf_op jit(solution)/shard_map/ppermute | solution.py:230
  16.3 0.0 collective-permute-done.3
  16.3 3.1 %collective-permute-start.5 = (bf16[256,256]{1,0:T(8,128)(2,1)S(1)}, bf16[256,256]{1,0:T(8,128)(2,1)S(1)}, u32[]{:S(2)}, u32[]{:S(2)}) collective-permute-start(bf16[256,256]{1,0:T(8,128)(2,1)S(1)} %select_select_fusion.1), channel_id=1, source_target_pairs={{0,16},{8,24},{16,32},{24,40},{32,48},{40,56},{48,0},{56,8},{64,80... | collective-permute-start | bytes 393224 | tf_op jit(solution)/shard_map/ppermute | solution.py:238
  19.4 4.2 %collective-permute-start.6 = (bf16[256,256]{1,0:T(8,128)(2,1)S(1)}, bf16[256,256]{1,0:T(8,128)(2,1)S(1)}, u32[]{:S(2)}, u32[]{:S(2)}) collective-permute-start(bf16[256,256]{1,0:T(8,128)(2,1)S(1)} %select_select_fusion.1), channel_id=1, source_target_pairs={{0,32},{8,40},{16,48},{24,56},{32,0},{40,8},{48,16},{56,24},{64,96... | collective-permute-start | bytes 393224 | tf_op jit(solution)/shard_map/ppermute | solution.py:238
  23.6 2.4 %collective-permute-start.7 = (bf16[256,256]{1,0:T(8,128)(2,1)S(1)}, bf16[256,256]{1,0:T(8,128)(2,1)S(1)}, u32[]{:S(2)}, u32[]{:S(2)}) collective-permute-start(bf16[256,256]{1,0:T(8,128)(2,1)S(1)} %select_select_fusion.1), channel_id=1, source_target_pairs={{0,48},{8,56},{16,0},{24,8},{32,16},{40,24},{48,32},{56,40},{64,11... | collective-permute-start | bytes 393224 | tf_op jit(solution)/shard_map/ppermute | solution.py:238
  26.0 0.8 pad_maximum_fusion
  26.8 0.0 collective-permute-done.8.refs_2_
  26.8 2.7 %collective-permute-start.13 = (bf16[256,1024]{1,0:T(8,128)(2,1)}, bf16[256,1024]{1,0:T(8,128)(2,1)S(1)}, u32[]{:S(2)}, u32[]{:S(2)}) collective-permute-start(bf16[256,1024]{1,0:T(8,128)(2,1)} %pad_maximum_fusion), channel_id=1, source_target_pairs={{0,4},{1,5},{2,6},{3,7},{4,0},{5,1},{6,2},{7,3},{8,12},{9,13},{10,... | collective-permute-start | bytes 1572872 | tf_op jit(solution)/shard_map/ppermute | solution.py:237
  29.5 0.0 copy-done.7
  29.5 0.1 reshape.17.queries
  29.6 0.0 copy-done.4
  29.7 0.0 copy-start
  29.7 2.2 %copy-done = bf16[32,256,256]{2,1,0:T(8,128)(2,1)S(1)} copy-done((bf16[32,256,256]{2,1,0:T(8,128)(2,1)S(1)}, bf16[32,256,256]{2,1,0:T(8,128)(2,1)}, u32[]{:S(2)}) %copy-start) | copy-done | bytes 4194328
  31.8 0.0 copy-start.8
  31.8 2.2 %shard_map.100 = (f32[1024,256]{1,0:T(8,128)S(1)}, f32[1024,1]{1,0:T(8,128)S(1)}) custom-call(s32[32]{0:T(128)S(1)} %copy-done.4, bf16[1024,128]{1,0:T(8,128)(2,1)S(1)} %reshape.17.queries, bf16[32,256,256]{2,1,0:T(8,128)(2,1)S(1)} %copy-done), custom_call_target="tpu_custom_call" | custom-call | flops 134217728 | bytes 4194304 | tf_op jit(solution)/shard_map/pallas_call | solution.py:82
  34.1 0.0 copy-start.5
  34.1 1.0 %copy-done.5 = f32[1024,256]{1,0:T(8,128)} copy-done((f32[1024,256]{1,0:T(8,128)}, f32[1024,256]{1,0:T(8,128)S(1)}, u32[]{:S(2)}) %copy-start.5) | copy-done | bytes 1048600
  35.1 0.0 collective-permute-done.9.refs_3_
  35.1 0.3 collective-permute-start.11
  35.4 0.0 collective-permute-done.5
  35.4 2.4 %collective-permute-start.12 = (bf16[128,1024]{1,0:T(8,128)(2,1)S(1)}, bf16[128,1024]{1,0:T(8,128)(2,1)S(1)}, u32[]{:S(2)}, u32[]{:S(2)}) collective-permute-start(bf16[128,1024]{1,0:T(8,128)(2,1)S(1)} %collective-permute-done.4.refs_1_), channel_id=1, source_target_pairs={{0,6},{1,7},{2,0},{3,1},{4,2},{5,3},{6,4},{7,5},{8,14},{9,15},{10,... | collective-permute-start | bytes 786440 | tf_op jit(solution)/shard_map/ppermute | solution.py:236
  37.8 0.0 collective-permute-done.6
  37.8 0.0 collective-permute-done.7
  37.8 1.0 %collective-permute-start.10 = (bf16[256,256]{1,0:T(8,128)(2,1)S(1)}, bf16[256,256]{1,0:T(8,128)(2,1)S(1)}, u32[]{:S(2)}, u32[]{:S(2)}) collective-permute-start(bf16[256,256]{1,0:T(8,128)(2,1)S(1)} %select_select_fusion), channel_id=1, source_target_pairs={{0,64},{8,72},{16,80},{24,88},{32,96},{40,104},{48,112},{56,120},{... | collective-permute-start | bytes 393224 | tf_op jit(solution)/shard_map/ppermute | solution.py:244
  38.8 2.3 %collective-permute-start.14 = (bf16[256,256]{1,0:T(8,128)(2,1)S(1)}, bf16[256,256]{1,0:T(8,128)(2,1)S(1)}, u32[]{:S(2)}, u32[]{:S(2)}) collective-permute-start(bf16[256,256]{1,0:T(8,128)(2,1)S(1)} %select_select_fusion), channel_id=1, source_target_pairs={{0,128},{8,136},{16,144},{24,152},{32,160},{40,168},{48,176},{56,1... | collective-permute-start | bytes 393224 | tf_op jit(solution)/shard_map/ppermute | solution.py:244
  41.0 2.2 %collective-permute-done.10 = bf16[256,256]{1,0:T(8,128)(2,1)S(1)} collective-permute-done((bf16[256,256]{1,0:T(8,128)(2,1)S(1)}, bf16[256,256]{1,0:T(8,128)(2,1)S(1)}, u32[]{:S(2)}, u32[]{:S(2)}) %collective-permute-start.10) | collective-permute-done | bytes 131104 | tf_op jit(solution)/shard_map/ppermute | solution.py:244
  43.2 0.8 collective-permute-start.15
  44.0 3.1 %collective-permute-done.11.refs_4_ = bf16[128,1024]{1,0:T(8,128)(2,1)S(1)} collective-permute-done((bf16[128,1024]{1,0:T(8,128)(2,1)S(1)}, bf16[128,1024]{1,0:T(8,128)(2,1)S(1)}, u32[]{:S(2)}, u32[]{:S(2)}) %collective-permute-start.11) | collective-permute-done | bytes 262176 | tf_op jit(solution)/shard_map/ppermute | solution.py:235
  47.1 0.0 collective-permute-done.12.refs_5_
  47.1 0.0 collective-permute-done.13.refs_6_
  47.1 0.0 collective-permute-done.14
  47.1 1.3 %collective-permute-done.15 = bf16[256,256]{1,0:T(8,128)(2,1)S(1)} collective-permute-done((bf16[256,256]{1,0:T(8,128)(2,1)S(1)}, bf16[256,256]{1,0:T(8,128)(2,1)S(1)}, u32[]{:S(2)}, u32[]{:S(2)}) %collective-permute-start.15) | collective-permute-done | bytes 131104 | tf_op jit(solution)/shard_map/ppermute | solution.py:244
  48.4 3.6 %collective-permute-start.16 = (bf16[1024,256]{1,0:T(8,128)(2,1)S(1)}, bf16[1024,256]{1,0:T(8,128)(2,1)}, u32[]{:S(2)}, u32[]{:S(2)}) collective-permute-start(bf16[1024,256]{1,0:T(8,128)(2,1)S(1)} %pad_maximum_fusion.1.key_values), channel_id=1, source_target_pairs={{0,8},{8,0},{16,24},{24,16},{32,40},{40,32},{48,56},{56,48},{64,72... | collective-permute-start | bytes 1572872 | tf_op jit(solution)/shard_map/ppermute | solution.py:248
  52.0 0.1 stack.35.owners
  52.1 0.0 copy-done.8
  52.1 0.2 convert_reduce_fusion
  52.3 0.0 copy-start.6
  52.3 1.2 %copy-done.6 = f32[1024,256]{1,0:T(8,128)S(1)} copy-done((f32[1024,256]{1,0:T(8,128)S(1)}, f32[1024,256]{1,0:T(8,128)}, u32[]{:S(2)}) %copy-start.6) | copy-done | bytes 1048600
  53.5 0.0 copy-start.2
  53.5 1.8 %shard_map.101 = (f32[1024,256]{1,0:T(8,128)S(1)}, f32[1024,1]{1,0:T(8,128)S(1)}) custom-call(bf16[1024,128]{1,0:T(8,128)(2,1)S(1)} %reshape.17.queries, bf16[1024,256]{1,0:T(8,128)(2,1)S(1)} %pad_maximum_fusion.1.key_values, f32[1024,256]{1,0:T(8,128)S(1)} %copy-done.6, f32[1024,1]{1,0:T(8,128)S(1)} %get-tuple-element.39.tops), custom_call_target="tpu_custom_call" | custom-call | flops 1073741824 | bytes 524288 | tf_op jit(solution)/shard_map/pallas_call | solution.py:115
  55.3 0.0 copy-start.1
  55.3 0.0 copy-start.3
  55.3 0.0 collective-permute-done.16.key_values
  55.3 2.9 %shard_map.102 = (f32[1024,256]{1,0:T(8,128)S(1)}, f32[1024,1]{1,0:T(8,128)S(1)}) custom-call(bf16[1024,128]{1,0:T(8,128)(2,1)S(1)} %reshape.17.queries, bf16[1024,256]{1,0:T(8,128)(2,1)} %collective-permute-done.16.key_values, f32[1024,256]{1,0:T(8,128)S(1)} %get-tuple-element.40.sums, f32[1024,1]{1,0:T(8,128)S(1)} %get-tuple-element.41.tops), custom_call_target="tpu_custom_call" | custom-call | flops 1073741824 | bytes 524288 | tf_op jit(solution)/shard_map/pallas_call | solution.py:115
  58.3 0.0 copy-done.2
  58.3 0.0 copy-done.1
  58.3 0.0 copy-done.3
  58.3 3.7 %shard_map.103 = bf16[64,32,128]{2,1,0:T(8,128)(2,1)S(1)} custom-call(s32[32]{0:T(128)S(1)} %multiply_add_fusion.slots, s32[8]{0:T(128)S(1)} %stack.35.owners, f32[1,8192]{1,0:T(1,128)S(1)} %bitcast.18, bf16[8192,128]{1,0:T(8,128)(2,1)S(1)} %copy-done.1, bf16[8192,128]{1,0:T(8,128)(2,1)S(1)} %copy-done.2, bf16[1024,128]{1,0:T(8,128)(2,1)S(1)} %reshape.17.queries, ...), custom_call_target="tpu_custom_call" | custom-call | flops 536870912 | bytes 4194304 | tf_op jit(solution)/shard_map/pallas_call | solution.py:181
  62.0 23.0 %all_to_all.5 = bf16[32,64,128]{2,1,0:T(8,128)(2,1)S(1)} all-to-all(bf16[32,64,128]{2,1,0:T(8,128)(2,1)S(1)} %bitcast.17), channel_id=1, replica_groups=mesh['dp'=32,'tensor'=8] {'dp'}, dimensions={0} | all-to-all | bytes 1048576 | tf_op jit(solution)/shard_map/all_to_all | solution.py:255
  85.0 0.9 %reshape.20 = bf16[64,4,1024]{2,1,0:T(4,128)(2,1)} reshape(bf16[32,64,128]{2,1,0:T(8,128)(2,1)S(1)} %all_to_all.5) | data formatting | bytes 1048576 | tf_op jit(solution)/shard_map/reshape | solution.py:258
  (5 shorter events, 0.1 us)
Async XLA Ops:
  0.0 5.7 %collective-permute-start = (bf16[2048,256]{1,0:T(8,128)(2,1)}, bf16[2048,256]{1,0:T(8,128)(2,1)S(1)}, u32[]{:S(2)}, u32[]{:S(2)}) collective-permute-start(bf16[2048,256]{1,0:T(8,128)(2,1)} %param.10), channel_id=1, source_target_pairs={{0,8},{8,0},{16,24},{24,16},{32,40},{40,32},{48,56},{56,48},{64,72... | collective-permute-start | bytes 3145736 | tf_op jit(solution)/shard_map/ppermute | solution.py:223
  4.3 8.2 %collective-permute-start.4 = (bf16[128,1024]{1,0:T(8,128)(2,1)S(1)}, bf16[128,1024]{1,0:T(8,128)(2,1)S(1)}, u32[]{:S(2)}, u32[]{:S(2)}) collective-permute-start(bf16[128,1024]{1,0:T(8,128)(2,1)S(1)} %reshape.18.refs_0_), channel_id=1, source_target_pairs={{0,1},{1,0},{2,3},{3,2},{4,5},{5,4},{6,7},{7,6},{8,9},{9,8},{10,11... | collective-permute-start | bytes 786440 | tf_op jit(solution)/shard_map/ppermute | solution.py:224
  5.0 24.5 %copy-start.7 = (bf16[32,4,1024]{2,1,0:T(4,128)(2,1)S(1)}, bf16[32,4,1024]{2,1,0:T(4,128)(2,1)}, u32[]{:S(2)}) copy-start(bf16[32,4,1024]{2,1,0:T(4,128)(2,1)} %param.19) | copy-start | bytes 786436
  6.8 22.8 %copy-start.4 = (s32[32]{0:T(128)S(1)}, s32[32]{0:T(128)}, u32[]{:S(2)}) copy-start(s32[32]{0:T(128)} %lengths.1) | copy-start | bytes 388
  6.9 7.0 %collective-permute-start.1 = (bf16[256,256]{1,0:T(8,128)(2,1)S(1)}, bf16[256,256]{1,0:T(8,128)(2,1)S(1)}, u32[]{:S(2)}, u32[]{:S(2)}) collective-permute-start(bf16[256,256]{1,0:T(8,128)(2,1)S(1)} %get-tuple-element.51), channel_id=1, source_target_pairs={{0,64},{8,72},{16,80},{24,88},{32,96},{40,104},{48,112},{56,120},{... | collective-permute-start | bytes 393224 | tf_op jit(solution)/shard_map/ppermute | solution.py:230
  7.5 8.8 %collective-permute-start.2 = (bf16[256,256]{1,0:T(8,128)(2,1)S(1)}, bf16[256,256]{1,0:T(8,128)(2,1)S(1)}, u32[]{:S(2)}, u32[]{:S(2)}) collective-permute-start(bf16[256,256]{1,0:T(8,128)(2,1)S(1)} %get-tuple-element.50), channel_id=1, source_target_pairs={{0,128},{8,136},{16,144},{24,152},{32,160},{40,168},{48,176},{56,1... | collective-permute-start | bytes 393224 | tf_op jit(solution)/shard_map/ppermute | solution.py:230
  10.1 6.2 %collective-permute-start.3 = (bf16[256,256]{1,0:T(8,128)(2,1)S(1)}, bf16[256,256]{1,0:T(8,128)(2,1)S(1)}, u32[]{:S(2)}, u32[]{:S(2)}) collective-permute-start(bf16[256,256]{1,0:T(8,128)(2,1)S(1)} %get-tuple-element.49), channel_id=1, source_target_pairs={{0,192},{8,200},{16,208},{24,216},{32,224},{40,232},{48,240},{56,2... | collective-permute-start | bytes 393224 | tf_op jit(solution)/shard_map/ppermute | solution.py:230
  11.2 15.6 %collective-permute-start.8 = (bf16[128,1024]{1,0:T(8,128)(2,1)S(1)}, bf16[128,1024]{1,0:T(8,128)(2,1)S(1)}, u32[]{:S(2)}, u32[]{:S(2)}) collective-permute-start(bf16[128,1024]{1,0:T(8,128)(2,1)S(1)} %reshape.18.refs_0_), channel_id=1, source_target_pairs={{0,2},{1,3},{2,4},{3,5},{4,6},{5,7},{6,0},{7,1},{8,10},{9,11},{10,... | collective-permute-start | bytes 786440 | tf_op jit(solution)/shard_map/ppermute | solution.py:225
  12.4 22.7 %collective-permute-start.9 = (bf16[128,1024]{1,0:T(8,128)(2,1)S(1)}, bf16[128,1024]{1,0:T(8,128)(2,1)S(1)}, u32[]{:S(2)}, u32[]{:S(2)}) collective-permute-start(bf16[128,1024]{1,0:T(8,128)(2,1)S(1)} %reshape.18.refs_0_), channel_id=1, source_target_pairs={{0,6},{1,7},{2,0},{3,1},{4,2},{5,3},{6,4},{7,5},{8,14},{9,15},{10,... | collective-permute-start | bytes 786440 | tf_op jit(solution)/shard_map/ppermute | solution.py:226
  16.3 19.1 %collective-permute-start.5 = (bf16[256,256]{1,0:T(8,128)(2,1)S(1)}, bf16[256,256]{1,0:T(8,128)(2,1)S(1)}, u32[]{:S(2)}, u32[]{:S(2)}) collective-permute-start(bf16[256,256]{1,0:T(8,128)(2,1)S(1)} %select_select_fusion.1), channel_id=1, source_target_pairs={{0,16},{8,24},{16,32},{24,40},{32,48},{40,56},{48,0},{56,8},{64,80... | collective-permute-start | bytes 393224 | tf_op jit(solution)/shard_map/ppermute | solution.py:238
  19.4 18.4 %collective-permute-start.6 = (bf16[256,256]{1,0:T(8,128)(2,1)S(1)}, bf16[256,256]{1,0:T(8,128)(2,1)S(1)}, u32[]{:S(2)}, u32[]{:S(2)}) collective-permute-start(bf16[256,256]{1,0:T(8,128)(2,1)S(1)} %select_select_fusion.1), channel_id=1, source_target_pairs={{0,32},{8,40},{16,48},{24,56},{32,0},{40,8},{48,16},{56,24},{64,96... | collective-permute-start | bytes 393224 | tf_op jit(solution)/shard_map/ppermute | solution.py:238
  23.6 14.2 %collective-permute-start.7 = (bf16[256,256]{1,0:T(8,128)(2,1)S(1)}, bf16[256,256]{1,0:T(8,128)(2,1)S(1)}, u32[]{:S(2)}, u32[]{:S(2)}) collective-permute-start(bf16[256,256]{1,0:T(8,128)(2,1)S(1)} %select_select_fusion.1), channel_id=1, source_target_pairs={{0,48},{8,56},{16,0},{24,8},{32,16},{40,24},{48,32},{56,40},{64,11... | collective-permute-start | bytes 393224 | tf_op jit(solution)/shard_map/ppermute | solution.py:238
  26.8 20.3 %collective-permute-start.13 = (bf16[256,1024]{1,0:T(8,128)(2,1)}, bf16[256,1024]{1,0:T(8,128)(2,1)S(1)}, u32[]{:S(2)}, u32[]{:S(2)}) collective-permute-start(bf16[256,1024]{1,0:T(8,128)(2,1)} %pad_maximum_fusion), channel_id=1, source_target_pairs={{0,4},{1,5},{2,6},{3,7},{4,0},{5,1},{6,2},{7,3},{8,12},{9,13},{10,... | collective-permute-start | bytes 1572872 | tf_op jit(solution)/shard_map/ppermute | solution.py:237
  29.7 2.2 %copy-start = (bf16[32,256,256]{2,1,0:T(8,128)(2,1)S(1)}, bf16[32,256,256]{2,1,0:T(8,128)(2,1)}, u32[]{:S(2)}) copy-start(bf16[32,256,256]{2,1,0:T(8,128)(2,1)} %pages.1) | copy-start | bytes 12582916
  31.8 20.2 %copy-start.8 = (s32[32,1]{0,1:T(1,128)S(1)}, s32[32,1]{0,1:T(1,128)}, u32[]{:S(2)}) copy-start(s32[32,1]{0,1:T(1,128)} %param.14) | copy-start | bytes 388
  34.1 1.0 %copy-start.5 = (f32[1024,256]{1,0:T(8,128)}, f32[1024,256]{1,0:T(8,128)S(1)}, u32[]{:S(2)}) copy-start(f32[1024,256]{1,0:T(8,128)S(1)} %get-tuple-element.38.sums) | copy-start | bytes 3145732
  35.1 12.0 %collective-permute-start.11 = (bf16[128,1024]{1,0:T(8,128)(2,1)S(1)}, bf16[128,1024]{1,0:T(8,128)(2,1)S(1)}, u32[]{:S(2)}, u32[]{:S(2)}) collective-permute-start(bf16[128,1024]{1,0:T(8,128)(2,1)S(1)} %collective-permute-done.4.refs_1_), channel_id=1, source_target_pairs={{0,2},{1,3},{2,4},{3,5},{4,6},{5,7},{6,0},{7,1},{8,10},{9,11},{10,... | collective-permute-start | bytes 786440 | tf_op jit(solution)/shard_map/ppermute | solution.py:235
  35.4 11.7 %collective-permute-start.12 = (bf16[128,1024]{1,0:T(8,128)(2,1)S(1)}, bf16[128,1024]{1,0:T(8,128)(2,1)S(1)}, u32[]{:S(2)}, u32[]{:S(2)}) collective-permute-start(bf16[128,1024]{1,0:T(8,128)(2,1)S(1)} %collective-permute-done.4.refs_1_), channel_id=1, source_target_pairs={{0,6},{1,7},{2,0},{3,1},{4,2},{5,3},{6,4},{7,5},{8,14},{9,15},{10,... | collective-permute-start | bytes 786440 | tf_op jit(solution)/shard_map/ppermute | solution.py:236
  37.8 5.4 %collective-permute-start.10 = (bf16[256,256]{1,0:T(8,128)(2,1)S(1)}, bf16[256,256]{1,0:T(8,128)(2,1)S(1)}, u32[]{:S(2)}, u32[]{:S(2)}) collective-permute-start(bf16[256,256]{1,0:T(8,128)(2,1)S(1)} %select_select_fusion), channel_id=1, source_target_pairs={{0,64},{8,72},{16,80},{24,88},{32,96},{40,104},{48,112},{56,120},{... | collective-permute-start | bytes 393224 | tf_op jit(solution)/shard_map/ppermute | solution.py:244
  38.8 8.3 %collective-permute-start.14 = (bf16[256,256]{1,0:T(8,128)(2,1)S(1)}, bf16[256,256]{1,0:T(8,128)(2,1)S(1)}, u32[]{:S(2)}, u32[]{:S(2)}) collective-permute-start(bf16[256,256]{1,0:T(8,128)(2,1)S(1)} %select_select_fusion), channel_id=1, source_target_pairs={{0,128},{8,136},{16,144},{24,152},{32,160},{40,168},{48,176},{56,1... | collective-permute-start | bytes 393224 | tf_op jit(solution)/shard_map/ppermute | solution.py:244
  43.2 5.2 %collective-permute-start.15 = (bf16[256,256]{1,0:T(8,128)(2,1)S(1)}, bf16[256,256]{1,0:T(8,128)(2,1)S(1)}, u32[]{:S(2)}, u32[]{:S(2)}) collective-permute-start(bf16[256,256]{1,0:T(8,128)(2,1)S(1)} %select_select_fusion), channel_id=1, source_target_pairs={{0,192},{8,200},{16,208},{24,216},{32,224},{40,232},{48,240},{56,2... | collective-permute-start | bytes 393224 | tf_op jit(solution)/shard_map/ppermute | solution.py:244
  48.4 6.9 %collective-permute-start.16 = (bf16[1024,256]{1,0:T(8,128)(2,1)S(1)}, bf16[1024,256]{1,0:T(8,128)(2,1)}, u32[]{:S(2)}, u32[]{:S(2)}) collective-permute-start(bf16[1024,256]{1,0:T(8,128)(2,1)S(1)} %pad_maximum_fusion.1.key_values), channel_id=1, source_target_pairs={{0,8},{8,0},{16,24},{24,16},{32,40},{40,32},{48,56},{56,48},{64,72... | collective-permute-start | bytes 1572872 | tf_op jit(solution)/shard_map/ppermute | solution.py:248
  52.3 1.2 %copy-start.6 = (f32[1024,256]{1,0:T(8,128)S(1)}, f32[1024,256]{1,0:T(8,128)}, u32[]{:S(2)}) copy-start(f32[1024,256]{1,0:T(8,128)} %copy-done.5) | copy-start | bytes 3145732
  53.5 4.8 %copy-start.2 = (bf16[8192,128]{1,0:T(8,128)(2,1)S(1)}, bf16[8192,128]{1,0:T(8,128)(2,1)}, u32[]{:S(2)}) copy-start(bf16[8192,128]{1,0:T(8,128)(2,1)} %value_weight.1) | copy-start | bytes 6291460
  55.3 3.0 %copy-start.1 = (bf16[8192,128]{1,0:T(8,128)(2,1)S(1)}, bf16[8192,128]{1,0:T(8,128)(2,1)}, u32[]{:S(2)}) copy-start(bf16[8192,128]{1,0:T(8,128)(2,1)} %key_weight.1) | copy-start | bytes 6291460
  55.3 3.0 %copy-start.3 = (f32[8192]{0:T(1024)S(1)}, f32[8192]{0:T(1024)}, u32[]{:S(2)}) copy-start(f32[8192]{0:T(1024)} %param.16) | copy-start | bytes 98308

commit v4 on v3

--- a/solution.py
+++ b/solution.py
@@ -242,7 +242,7 @@
     places = [(0, 0), (0, 1), (X - 1, 0), (1, 0), (X - 1, 1), (1, 1), (2, 0), (2, 1)]
     owners = jnp.stack([(x + dx) % X * PAIR + (pair ^ flip) for dx, flip in places]).astype(jnp.int32)
     arrived = [part] + [lax.ppermute(part, "dp", y_step(k)) for k in range(1, Y)]
-    arrived[1], twin_left, twin_right, far = together(arrived[1], twin_left, twin_right, far)
+    arrived[3], twin_left, twin_right, far = together(arrived[3], twin_left, twin_right, far)
     blocks = [block, twin, left, right, twin_left, twin_right, far]
     near = jnp.concatenate(arrived)
     far_prefix = lax.ppermute(near, "dp", core_swap())

time: 86.2 us -> 86.4 us (level)
  no operation moved by 1% of the time
where the time goes in v4:
time: 86.4 us; the launch traced here: 86.1 us
  starting transfers between devices  33.2 us (38%)
  blocking collectives  22.9 us (27%)
  Pallas kernels  10.6 us (12%)
  waiting for transfers between devices  9.7 us (11%)
  local copies, waits for them, and re-layouts  6.61 us (8%)
  other arithmetic  2.21 us (3%)
    all_to_all x1, blocking collectives, per_device(): lax.all_to_all(result.reshape(group_count, CAP * 32, HEAD_SIZE), 'dp', sp...  22.9 us
    ppermute x3, starting transfers between devices, per_device(): lax.ppermute(part, 'dp', z_step(k))  9.62 us
    pallas_call x2, Pallas kernels, prefix_part(): pl.pallas_call(prefix_kernel, in_specs=[vmem] * 4, out_specs=[vmem] * 2,...  4.74 us
    unnamed x18, local copies, waits for them, and re-layouts  4.46 us
    ppermute x3, starting transfers between devices, per_device(): lax.ppermute(mine[piece * k:piece * (k + 1)], 'dp', y_step(k))  4.31 us
    ppermute x3, starting transfers between devices, per_device(): lax.ppermute(part, 'dp', y_step(k))  4.08 us
    ppermute x1, starting transfers between devices, per_device(): far_prefix = lax.ppermute(near, 'dp', core_swap())  3.75 us
    pallas_call x1, Pallas kernels, finish(): pl.pallas_call(finish_kernel, in_specs=[smem, smem] + [vmem] * (6 + len(b...  3.68 us
  transfers between devices with their start and end apart: 17, of which 5 were waited for; matrix products, arithmetic and copies ran while one was open for 4% of the time, Pallas kernels for 5%

profile of v4, /device:TPU:1, one launch (start us, length us, event | category | flops | bytes accessed | tf_op | source)
XLA Modules:
  0.0 86.1 jit_solution(6410740946865609420)
XLA Ops:
  0.0 3.2 %collective-permute-start = (bf16[2048,256]{1,0:T(8,128)(2,1)}, bf16[2048,256]{1,0:T(8,128)(2,1)S(1)}, u32[]{:S(2)}, u32[]{:S(2)}) collective-permute-start(bf16[2048,256]{1,0:T(8,128)(2,1)} %param.10), channel_id=1, source_target_pairs={{0,8},{8,0},{16,24},{24,16},{32,40},{40,32},{48,56},{56,48},{64,72... | collective-permute-start | bytes 3145736 | tf_op jit(solution)/shard_map/ppermute | solution.py:223
  3.2 1.0 %reshape.18.refs_0_ = bf16[128,1024]{1,0:T(8,128)(2,1)S(1)} reshape(bf16[32,4,1024]{2,1,0:T(4,128)(2,1)} %param.15) | data formatting | bytes 524288 | tf_op jit(solution)/shard_map/reshape | solution.py:221
  4.3 0.1 collective-permute-start.4
  5.0 0.0 copy-start.7
  5.1 0.7 collective-permute-done
  5.7 1.1 %slice_select_fusion = bf16[1024,256]{1,0:T(8,128)(2,1)S(1)} fusion(bf16[2048,256]{1,0:T(8,128)(2,1)S(1)} %collective-permute-done, bf16[2048,256]{1,0:T(8,128)(2,1)} %param.10, pred[]{:T(512)S(6)} %eq.55), kind=kLoop, calls=%fused_computation | loop fusion | flops 262144 | bytes 1572865 | tf_op jit(solution)/shard_map/jit(_where)/select_n | solution.py:227
  6.8 0.0 copy-start.4
  6.9 0.6 collective-permute-start.1
  7.5 2.6 %collective-permute-start.2 = (bf16[256,256]{1,0:T(8,128)(2,1)S(1)}, bf16[256,256]{1,0:T(8,128)(2,1)S(1)}, u32[]{:S(2)}, u32[]{:S(2)}) collective-permute-start(bf16[256,256]{1,0:T(8,128)(2,1)S(1)} %get-tuple-element.50), channel_id=1, source_target_pairs={{0,128},{8,136},{16,144},{24,152},{32,160},{40,168},{48,176},{56,1... | collective-permute-start | bytes 393224 | tf_op jit(solution)/shard_map/ppermute | solution.py:230
  10.1 1.1 %collective-permute-start.3 = (bf16[256,256]{1,0:T(8,128)(2,1)S(1)}, bf16[256,256]{1,0:T(8,128)(2,1)S(1)}, u32[]{:S(2)}, u32[]{:S(2)}) collective-permute-start(bf16[256,256]{1,0:T(8,128)(2,1)S(1)} %get-tuple-element.49), channel_id=1, source_target_pairs={{0,192},{8,200},{16,208},{24,216},{32,224},{40,232},{48,240},{56,2... | collective-permute-start | bytes 393224 | tf_op jit(solution)/shard_map/ppermute | solution.py:230
  11.2 1.2 %collective-permute-start.8 = (bf16[128,1024]{1,0:T(8,128)(2,1)S(1)}, bf16[128,1024]{1,0:T(8,128)(2,1)S(1)}, u32[]{:S(2)}, u32[]{:S(2)}) collective-permute-start(bf16[128,1024]{1,0:T(8,128)(2,1)S(1)} %reshape.18.refs_0_), channel_id=1, source_target_pairs={{0,2},{1,3},{2,4},{3,5},{4,6},{5,7},{6,0},{7,1},{8,10},{9,11},{10,... | collective-permute-start | bytes 786440 | tf_op jit(solution)/shard_map/ppermute | solution.py:225
  12.4 0.0 collective-permute-done.4.refs_1_
  12.4 1.5 %collective-permute-start.9 = (bf16[128,1024]{1,0:T(8,128)(2,1)S(1)}, bf16[128,1024]{1,0:T(8,128)(2,1)S(1)}, u32[]{:S(2)}, u32[]{:S(2)}) collective-permute-start(bf16[128,1024]{1,0:T(8,128)(2,1)S(1)} %reshape.18.refs_0_), channel_id=1, source_target_pairs={{0,6},{1,7},{2,0},{3,1},{4,2},{5,3},{6,4},{7,5},{8,14},{9,15},{10,... | collective-permute-start | bytes 786440 | tf_op jit(solution)/shard_map/ppermute | solution.py:226
  13.9 0.0 collective-permute-done.1
  13.9 2.4 %collective-permute-done.2 = bf16[256,256]{1,0:T(8,128)(2,1)S(1)} collective-permute-done((bf16[256,256]{1,0:T(8,128)(2,1)S(1)}, bf16[256,256]{1,0:T(8,128)(2,1)S(1)}, u32[]{:S(2)}, u32[]{:S(2)}) %collective-permute-start.2) | collective-permute-done | bytes 131104 | tf_op jit(solution)/shard_map/ppermute | solution.py:230
  16.3 0.0 collective-permute-done.3
  16.3 3.1 %collective-permute-start.5 = (bf16[256,256]{1,0:T(8,128)(2,1)S(1)}, bf16[256,256]{1,0:T(8,128)(2,1)S(1)}, u32[]{:S(2)}, u32[]{:S(2)}) collective-permute-start(bf16[256,256]{1,0:T(8,128)(2,1)S(1)} %select_select_fusion.1), channel_id=1, source_target_pairs={{0,16},{8,24},{16,32},{24,40},{32,48},{40,56},{48,0},{56,8},{64,80... | collective-permute-start | bytes 393224 | tf_op jit(solution)/shard_map/ppermute | solution.py:238
  19.4 4.2 %collective-permute-start.6 = (bf16[256,256]{1,0:T(8,128)(2,1)S(1)}, bf16[256,256]{1,0:T(8,128)(2,1)S(1)}, u32[]{:S(2)}, u32[]{:S(2)}) collective-permute-start(bf16[256,256]{1,0:T(8,128)(2,1)S(1)} %select_select_fusion.1), channel_id=1, source_target_pairs={{0,32},{8,40},{16,48},{24,56},{32,0},{40,8},{48,16},{56,24},{64,96... | collective-permute-start | bytes 393224 | tf_op jit(solution)/shard_map/ppermute | solution.py:238
  23.6 2.4 %collective-permute-start.7 = (bf16[256,256]{1,0:T(8,128)(2,1)S(1)}, bf16[256,256]{1,0:T(8,128)(2,1)S(1)}, u32[]{:S(2)}, u32[]{:S(2)}) collective-permute-start(bf16[256,256]{1,0:T(8,128)(2,1)S(1)} %select_select_fusion.1), channel_id=1, source_target_pairs={{0,48},{8,56},{16,0},{24,8},{32,16},{40,24},{48,32},{56,40},{64,11... | collective-permute-start | bytes 393224 | tf_op jit(solution)/shard_map/ppermute | solution.py:238
  26.0 0.8 pad_maximum_fusion
  26.8 0.0 collective-permute-done.8.refs_2_
  26.8 2.7 %collective-permute-start.15 = (bf16[256,1024]{1,0:T(8,128)(2,1)}, bf16[256,1024]{1,0:T(8,128)(2,1)S(1)}, u32[]{:S(2)}, u32[]{:S(2)}) collective-permute-start(bf16[256,1024]{1,0:T(8,128)(2,1)} %pad_maximum_fusion), channel_id=1, source_target_pairs={{0,4},{1,5},{2,6},{3,7},{4,0},{5,1},{6,2},{7,3},{8,12},{9,13},{10,... | collective-permute-start | bytes 1572872 | tf_op jit(solution)/shard_map/ppermute | solution.py:237
  29.5 0.0 copy-done.7
  29.5 0.1 reshape.17.queries
  29.6 0.0 copy-done.4
  29.7 0.0 copy-start
  29.7 2.2 %copy-done = bf16[32,256,256]{2,1,0:T(8,128)(2,1)S(1)} copy-done((bf16[32,256,256]{2,1,0:T(8,128)(2,1)S(1)}, bf16[32,256,256]{2,1,0:T(8,128)(2,1)}, u32[]{:S(2)}) %copy-start) | copy-done | bytes 4194328
  31.8 0.0 copy-start.8
  31.8 2.2 %shard_map.100 = (f32[1024,256]{1,0:T(8,128)S(1)}, f32[1024,1]{1,0:T(8,128)S(1)}) custom-call(s32[32]{0:T(128)S(1)} %copy-done.4, bf16[1024,128]{1,0:T(8,128)(2,1)S(1)} %reshape.17.queries, bf16[32,256,256]{2,1,0:T(8,128)(2,1)S(1)} %copy-done), custom_call_target="tpu_custom_call" | custom-call | flops 134217728 | bytes 4194304 | tf_op jit(solution)/shard_map/pallas_call | solution.py:82
  34.1 0.0 copy-start.5
  34.1 1.0 %copy-done.5 = f32[1024,256]{1,0:T(8,128)} copy-done((f32[1024,256]{1,0:T(8,128)}, f32[1024,256]{1,0:T(8,128)S(1)}, u32[]{:S(2)}) %copy-start.5) | copy-done | bytes 1048600
  35.1 0.0 collective-permute-done.9.refs_3_
  35.1 0.3 collective-permute-start.13
  35.4 0.0 collective-permute-done.5
  35.4 2.4 %collective-permute-start.14 = (bf16[128,1024]{1,0:T(8,128)(2,1)S(1)}, bf16[128,1024]{1,0:T(8,128)(2,1)S(1)}, u32[]{:S(2)}, u32[]{:S(2)}) collective-permute-start(bf16[128,1024]{1,0:T(8,128)(2,1)S(1)} %collective-permute-done.4.refs_1_), channel_id=1, source_target_pairs={{0,6},{1,7},{2,0},{3,1},{4,2},{5,3},{6,4},{7,5},{8,14},{9,15},{10,... | collective-permute-start | bytes 786440 | tf_op jit(solution)/shard_map/ppermute | solution.py:236
  37.8 0.0 collective-permute-done.6
  37.8 0.0 collective-permute-done.7
  37.8 2.1 %collective-permute-start.12 = (bf16[256,256]{1,0:T(8,128)(2,1)S(1)}, bf16[256,256]{1,0:T(8,128)(2,1)S(1)}, u32[]{:S(2)}, u32[]{:S(2)}) collective-permute-start(bf16[256,256]{1,0:T(8,128)(2,1)S(1)} %select_select_fusion), channel_id=1, source_target_pairs={{0,192},{8,200},{16,208},{24,216},{32,224},{40,232},{48,240},{56,2... | collective-permute-start | bytes 393224 | tf_op jit(solution)/shard_map/ppermute | solution.py:244
  39.9 0.0 collective-permute-start.10
  39.9 2.1 %collective-permute-done.12 = bf16[256,256]{1,0:T(8,128)(2,1)S(1)} collective-permute-done((bf16[256,256]{1,0:T(8,128)(2,1)S(1)}, bf16[256,256]{1,0:T(8,128)(2,1)S(1)}, u32[]{:S(2)}, u32[]{:S(2)}) %collective-permute-start.12) | collective-permute-done | bytes 131104 | tf_op jit(solution)/shard_map/ppermute | solution.py:244
  42.0 2.0 %collective-permute-start.11 = (bf16[256,256]{1,0:T(8,128)(2,1)S(1)}, bf16[256,256]{1,0:T(8,128)(2,1)S(1)}, u32[]{:S(2)}, u32[]{:S(2)}) collective-permute-start(bf16[256,256]{1,0:T(8,128)(2,1)S(1)} %select_select_fusion), channel_id=1, source_target_pairs={{0,128},{8,136},{16,144},{24,152},{32,160},{40,168},{48,176},{56,1... | collective-permute-start | bytes 393224 | tf_op jit(solution)/shard_map/ppermute | solution.py:244
  44.0 3.1 %collective-permute-done.13.refs_4_ = bf16[128,1024]{1,0:T(8,128)(2,1)S(1)} collective-permute-done((bf16[128,1024]{1,0:T(8,128)(2,1)S(1)}, bf16[128,1024]{1,0:T(8,128)(2,1)S(1)}, u32[]{:S(2)}, u32[]{:S(2)}) %collective-permute-start.13) | collective-permute-done | bytes 262176 | tf_op jit(solution)/shard_map/ppermute | solution.py:235
  47.1 0.0 collective-permute-done.14.refs_5_
  47.1 0.0 collective-permute-done.15.refs_6_
  47.1 0.0 collective-permute-done.10
  47.1 1.4 %collective-permute-done.11 = bf16[256,256]{1,0:T(8,128)(2,1)S(1)} collective-permute-done((bf16[256,256]{1,0:T(8,128)(2,1)S(1)}, bf16[256,256]{1,0:T(8,128)(2,1)S(1)}, u32[]{:S(2)}, u32[]{:S(2)}) %collective-permute-start.11) | collective-permute-done | bytes 131104 | tf_op jit(solution)/shard_map/ppermute | solution.py:244
  48.5 3.8 %collective-permute-start.16 = (bf16[1024,256]{1,0:T(8,128)(2,1)S(1)}, bf16[1024,256]{1,0:T(8,128)(2,1)}, u32[]{:S(2)}, u32[]{:S(2)}) collective-permute-start(bf16[1024,256]{1,0:T(8,128)(2,1)S(1)} %pad_maximum_fusion.1.key_values), channel_id=1, source_target_pairs={{0,8},{8,0},{16,24},{24,16},{32,40},{40,32},{48,56},{56,48},{64,72... | collective-permute-start | bytes 1572872 | tf_op jit(solution)/shard_map/ppermute | solution.py:248
  52.3 0.1 stack.35.owners
  52.4 0.0 copy-done.8
  52.4 0.2 convert_reduce_fusion
  52.6 0.0 copy-start.6
  52.6 1.2 %copy-done.6 = f32[1024,256]{1,0:T(8,128)S(1)} copy-done((f32[1024,256]{1,0:T(8,128)S(1)}, f32[1024,256]{1,0:T(8,128)}, u32[]{:S(2)}) %copy-start.6) | copy-done | bytes 1048600
  53.8 0.0 copy-start.2
  53.8 1.8 %shard_map.101 = (f32[1024,256]{1,0:T(8,128)S(1)}, f32[1024,1]{1,0:T(8,128)S(1)}) custom-call(bf16[1024,128]{1,0:T(8,128)(2,1)S(1)} %reshape.17.queries, bf16[1024,256]{1,0:T(8,128)(2,1)S(1)} %pad_maximum_fusion.1.key_values, f32[1024,256]{1,0:T(8,128)S(1)} %copy-done.6, f32[1024,1]{1,0:T(8,128)S(1)} %get-tuple-element.39.tops), custom_call_target="tpu_custom_call" | custom-call | flops 1073741824 | bytes 524288 | tf_op jit(solution)/shard_map/pallas_call | solution.py:115
  55.6 0.0 copy-start.1
  55.6 0.0 copy-start.3
  55.6 0.0 collective-permute-done.16.key_values
  55.6 2.9 %shard_map.102 = (f32[1024,256]{1,0:T(8,128)S(1)}, f32[1024,1]{1,0:T(8,128)S(1)}) custom-call(bf16[1024,128]{1,0:T(8,128)(2,1)S(1)} %reshape.17.queries, bf16[1024,256]{1,0:T(8,128)(2,1)} %collective-permute-done.16.key_values, f32[1024,256]{1,0:T(8,128)S(1)} %get-tuple-element.40.sums, f32[1024,1]{1,0:T(8,128)S(1)} %get-tuple-element.41.tops), custom_call_target="tpu_custom_call" | custom-call | flops 1073741824 | bytes 524288 | tf_op jit(solution)/shard_map/pallas_call | solution.py:115
  58.6 0.0 copy-done.2
  58.6 0.0 copy-done.1
  58.6 0.0 copy-done.3
  58.6 3.7 %shard_map.103 = bf16[64,32,128]{2,1,0:T(8,128)(2,1)S(1)} custom-call(s32[32]{0:T(128)S(1)} %multiply_add_fusion.slots, s32[8]{0:T(128)S(1)} %stack.35.owners, f32[1,8192]{1,0:T(1,128)S(1)} %bitcast.18, bf16[8192,128]{1,0:T(8,128)(2,1)S(1)} %copy-done.1, bf16[8192,128]{1,0:T(8,128)(2,1)S(1)} %copy-done.2, bf16[1024,128]{1,0:T(8,128)(2,1)S(1)} %reshape.17.queries, ...), custom_call_target="tpu_custom_call" | custom-call | flops 536870912 | bytes 4194304 | tf_op jit(solution)/shard_map/pallas_call | solution.py:181
  62.3 22.9 %all_to_all.5 = bf16[32,64,128]{2,1,0:T(8,128)(2,1)S(1)} all-to-all(bf16[32,64,128]{2,1,0:T(8,128)(2,1)S(1)} %bitcast.17), channel_id=1, replica_groups=mesh['dp'=32,'tensor'=8] {'dp'}, dimensions={0} | all-to-all | bytes 1048576 | tf_op jit(solution)/shard_map/all_to_all | solution.py:255
  85.2 0.9 %reshape.20 = bf16[64,4,1024]{2,1,0:T(4,128)(2,1)} reshape(bf16[32,64,128]{2,1,0:T(8,128)(2,1)S(1)} %all_to_all.5) | data formatting | bytes 1048576 | tf_op jit(solution)/shard_map/reshape | solution.py:258
  (5 shorter events, 0.1 us)
Async XLA Ops:
  0.0 5.7 %collective-permute-start = (bf16[2048,256]{1,0:T(8,128)(2,1)}, bf16[2048,256]{1,0:T(8,128)(2,1)S(1)}, u32[]{:S(2)}, u32[]{:S(2)}) collective-permute-start(bf16[2048,256]{1,0:T(8,128)(2,1)} %param.10), channel_id=1, source_target_pairs={{0,8},{8,0},{16,24},{24,16},{32,40},{40,32},{48,56},{56,48},{64,72... | collective-permute-start | bytes 3145736 | tf_op jit(solution)/shard_map/ppermute | solution.py:223
  4.3 8.2 %collective-permute-start.4 = (bf16[128,1024]{1,0:T(8,128)(2,1)S(1)}, bf16[128,1024]{1,0:T(8,128)(2,1)S(1)}, u32[]{:S(2)}, u32[]{:S(2)}) collective-permute-start(bf16[128,1024]{1,0:T(8,128)(2,1)S(1)} %reshape.18.refs_0_), channel_id=1, source_target_pairs={{0,1},{1,0},{2,3},{3,2},{4,5},{5,4},{6,7},{7,6},{8,9},{9,8},{10,11... | collective-permute-start | bytes 786440 | tf_op jit(solution)/shard_map/ppermute | solution.py:224
  5.0 24.5 %copy-start.7 = (bf16[32,4,1024]{2,1,0:T(4,128)(2,1)S(1)}, bf16[32,4,1024]{2,1,0:T(4,128)(2,1)}, u32[]{:S(2)}) copy-start(bf16[32,4,1024]{2,1,0:T(4,128)(2,1)} %param.19) | copy-start | bytes 786436
  6.8 22.8 %copy-start.4 = (s32[32]{0:T(128)S(1)}, s32[32]{0:T(128)}, u32[]{:S(2)}) copy-start(s32[32]{0:T(128)} %lengths.1) | copy-start | bytes 388
  6.9 7.0 %collective-permute-start.1 = (bf16[256,256]{1,0:T(8,128)(2,1)S(1)}, bf16[256,256]{1,0:T(8,128)(2,1)S(1)}, u32[]{:S(2)}, u32[]{:S(2)}) collective-permute-start(bf16[256,256]{1,0:T(8,128)(2,1)S(1)} %get-tuple-element.51), channel_id=1, source_target_pairs={{0,64},{8,72},{16,80},{24,88},{32,96},{40,104},{48,112},{56,120},{... | collective-permute-start | bytes 393224 | tf_op jit(solution)/shard_map/ppermute | solution.py:230
  7.5 8.8 %collective-permute-start.2 = (bf16[256,256]{1,0:T(8,128)(2,1)S(1)}, bf16[256,256]{1,0:T(8,128)(2,1)S(1)}, u32[]{:S(2)}, u32[]{:S(2)}) collective-permute-start(bf16[256,256]{1,0:T(8,128)(2,1)S(1)} %get-tuple-element.50), channel_id=1, source_target_pairs={{0,128},{8,136},{16,144},{24,152},{32,160},{40,168},{48,176},{56,1... | collective-permute-start | bytes 393224 | tf_op jit(solution)/shard_map/ppermute | solution.py:230
  10.1 6.2 %collective-permute-start.3 = (bf16[256,256]{1,0:T(8,128)(2,1)S(1)}, bf16[256,256]{1,0:T(8,128)(2,1)S(1)}, u32[]{:S(2)}, u32[]{:S(2)}) collective-permute-start(bf16[256,256]{1,0:T(8,128)(2,1)S(1)} %get-tuple-element.49), channel_id=1, source_target_pairs={{0,192},{8,200},{16,208},{24,216},{32,224},{40,232},{48,240},{56,2... | collective-permute-start | bytes 393224 | tf_op jit(solution)/shard_map/ppermute | solution.py:230
  11.2 15.6 %collective-permute-start.8 = (bf16[128,1024]{1,0:T(8,128)(2,1)S(1)}, bf16[128,1024]{1,0:T(8,128)(2,1)S(1)}, u32[]{:S(2)}, u32[]{:S(2)}) collective-permute-start(bf16[128,1024]{1,0:T(8,128)(2,1)S(1)} %reshape.18.refs_0_), channel_id=1, source_target_pairs={{0,2},{1,3},{2,4},{3,5},{4,6},{5,7},{6,0},{7,1},{8,10},{9,11},{10,... | collective-permute-start | bytes 786440 | tf_op jit(solution)/shard_map/ppermute | solution.py:225
  12.4 22.7 %collective-permute-start.9 = (bf16[128,1024]{1,0:T(8,128)(2,1)S(1)}, bf16[128,1024]{1,0:T(8,128)(2,1)S(1)}, u32[]{:S(2)}, u32[]{:S(2)}) collective-permute-start(bf16[128,1024]{1,0:T(8,128)(2,1)S(1)} %reshape.18.refs_0_), channel_id=1, source_target_pairs={{0,6},{1,7},{2,0},{3,1},{4,2},{5,3},{6,4},{7,5},{8,14},{9,15},{10,... | collective-permute-start | bytes 786440 | tf_op jit(solution)/shard_map/ppermute | solution.py:226
  16.3 19.1 %collective-permute-start.5 = (bf16[256,256]{1,0:T(8,128)(2,1)S(1)}, bf16[256,256]{1,0:T(8,128)(2,1)S(1)}, u32[]{:S(2)}, u32[]{:S(2)}) collective-permute-start(bf16[256,256]{1,0:T(8,128)(2,1)S(1)} %select_select_fusion.1), channel_id=1, source_target_pairs={{0,16},{8,24},{16,32},{24,40},{32,48},{40,56},{48,0},{56,8},{64,80... | collective-permute-start | bytes 393224 | tf_op jit(solution)/shard_map/ppermute | solution.py:238
  19.4 18.4 %collective-permute-start.6 = (bf16[256,256]{1,0:T(8,128)(2,1)S(1)}, bf16[256,256]{1,0:T(8,128)(2,1)S(1)}, u32[]{:S(2)}, u32[]{:S(2)}) collective-permute-start(bf16[256,256]{1,0:T(8,128)(2,1)S(1)} %select_select_fusion.1), channel_id=1, source_target_pairs={{0,32},{8,40},{16,48},{24,56},{32,0},{40,8},{48,16},{56,24},{64,96... | collective-permute-start | bytes 393224 | tf_op jit(solution)/shard_map/ppermute | solution.py:238
  23.6 14.2 %collective-permute-start.7 = (bf16[256,256]{1,0:T(8,128)(2,1)S(1)}, bf16[256,256]{1,0:T(8,128)(2,1)S(1)}, u32[]{:S(2)}, u32[]{:S(2)}) collective-permute-start(bf16[256,256]{1,0:T(8,128)(2,1)S(1)} %select_select_fusion.1), channel_id=1, source_target_pairs={{0,48},{8,56},{16,0},{24,8},{32,16},{40,24},{48,32},{56,40},{64,11... | collective-permute-start | bytes 393224 | tf_op jit(solution)/shard_map/ppermute | solution.py:238
  26.8 20.3 %collective-permute-start.15 = (bf16[256,1024]{1,0:T(8,128)(2,1)}, bf16[256,1024]{1,0:T(8,128)(2,1)S(1)}, u32[]{:S(2)}, u32[]{:S(2)}) collective-permute-start(bf16[256,1024]{1,0:T(8,128)(2,1)} %pad_maximum_fusion), channel_id=1, source_target_pairs={{0,4},{1,5},{2,6},{3,7},{4,0},{5,1},{6,2},{7,3},{8,12},{9,13},{10,... | collective-permute-start | bytes 1572872 | tf_op jit(solution)/shard_map/ppermute | solution.py:237
  29.7 2.2 %copy-start = (bf16[32,256,256]{2,1,0:T(8,128)(2,1)S(1)}, bf16[32,256,256]{2,1,0:T(8,128)(2,1)}, u32[]{:S(2)}) copy-start(bf16[32,256,256]{2,1,0:T(8,128)(2,1)} %pages.1) | copy-start | bytes 12582916
  31.8 20.5 %copy-start.8 = (s32[32,1]{0,1:T(1,128)S(1)}, s32[32,1]{0,1:T(1,128)}, u32[]{:S(2)}) copy-start(s32[32,1]{0,1:T(1,128)} %param.14) | copy-start | bytes 388
  34.1 1.0 %copy-start.5 = (f32[1024,256]{1,0:T(8,128)}, f32[1024,256]{1,0:T(8,128)S(1)}, u32[]{:S(2)}) copy-start(f32[1024,256]{1,0:T(8,128)S(1)} %get-tuple-element.38.sums) | copy-start | bytes 3145732
  35.1 12.0 %collective-permute-start.13 = (bf16[128,1024]{1,0:T(8,128)(2,1)S(1)}, bf16[128,1024]{1,0:T(8,128)(2,1)S(1)}, u32[]{:S(2)}, u32[]{:S(2)}) collective-permute-start(bf16[128,1024]{1,0:T(8,128)(2,1)S(1)} %collective-permute-done.4.refs_1_), channel_id=1, source_target_pairs={{0,2},{1,3},{2,4},{3,5},{4,6},{5,7},{6,0},{7,1},{8,10},{9,11},{10,... | collective-permute-start | bytes 786440 | tf_op jit(solution)/shard_map/ppermute | solution.py:235
  35.4 11.7 %collective-permute-start.14 = (bf16[128,1024]{1,0:T(8,128)(2,1)S(1)}, bf16[128,1024]{1,0:T(8,128)(2,1)S(1)}, u32[]{:S(2)}, u32[]{:S(2)}) collective-permute-start(bf16[128,1024]{1,0:T(8,128)(2,1)S(1)} %collective-permute-done.4.refs_1_), channel_id=1, source_target_pairs={{0,6},{1,7},{2,0},{3,1},{4,2},{5,3},{6,4},{7,5},{8,14},{9,15},{10,... | collective-permute-start | bytes 786440 | tf_op jit(solution)/shard_map/ppermute | solution.py:236
  37.8 4.2 %collective-permute-start.12 = (bf16[256,256]{1,0:T(8,128)(2,1)S(1)}, bf16[256,256]{1,0:T(8,128)(2,1)S(1)}, u32[]{:S(2)}, u32[]{:S(2)}) collective-permute-start(bf16[256,256]{1,0:T(8,128)(2,1)S(1)} %select_select_fusion), channel_id=1, source_target_pairs={{0,192},{8,200},{16,208},{24,216},{32,224},{40,232},{48,240},{56,2... | collective-permute-start | bytes 393224 | tf_op jit(solution)/shard_map/ppermute | solution.py:244
  39.9 7.2 %collective-permute-start.10 = (bf16[256,256]{1,0:T(8,128)(2,1)S(1)}, bf16[256,256]{1,0:T(8,128)(2,1)S(1)}, u32[]{:S(2)}, u32[]{:S(2)}) collective-permute-start(bf16[256,256]{1,0:T(8,128)(2,1)S(1)} %select_select_fusion), channel_id=1, source_target_pairs={{0,64},{8,72},{16,80},{24,88},{32,96},{40,104},{48,112},{56,120},{... | collective-permute-start | bytes 393224 | tf_op jit(solution)/shard_map/ppermute | solution.py:244
  42.0 6.5 %collective-permute-start.11 = (bf16[256,256]{1,0:T(8,128)(2,1)S(1)}, bf16[256,256]{1,0:T(8,128)(2,1)S(1)}, u32[]{:S(2)}, u32[]{:S(2)}) collective-permute-start(bf16[256,256]{1,0:T(8,128)(2,1)S(1)} %select_select_fusion), channel_id=1, source_target_pairs={{0,128},{8,136},{16,144},{24,152},{32,160},{40,168},{48,176},{56,1... | collective-permute-start | bytes 393224 | tf_op jit(solution)/shard_map/ppermute | solution.py:244
  48.5 7.1 %collective-permute-start.16 = (bf16[1024,256]{1,0:T(8,128)(2,1)S(1)}, bf16[1024,256]{1,0:T(8,128)(2,1)}, u32[]{:S(2)}, u32[]{:S(2)}) collective-permute-start(bf16[1024,256]{1,0:T(8,128)(2,1)S(1)} %pad_maximum_fusion.1.key_values), channel_id=1, source_target_pairs={{0,8},{8,0},{16,24},{24,16},{32,40},{40,32},{48,56},{56,48},{64,72... | collective-permute-start | bytes 1572872 | tf_op jit(solution)/shard_map/ppermute | solution.py:248
  52.6 1.2 %copy-start.6 = (f32[1024,256]{1,0:T(8,128)S(1)}, f32[1024,256]{1,0:T(8,128)}, u32[]{:S(2)}) copy-start(f32[1024,256]{1,0:T(8,128)} %copy-done.5) | copy-start | bytes 3145732
  53.8 4.8 %copy-start.2 = (bf16[8192,128]{1,0:T(8,128)(2,1)S(1)}, bf16[8192,128]{1,0:T(8,128)(2,1)}, u32[]{:S(2)}) copy-start(bf16[8192,128]{1,0:T(8,128)(2,1)} %value_weight.1) | copy-start | bytes 6291460
  55.6 3.0 %copy-start.1 = (bf16[8192,128]{1,0:T(8,128)(2,1)S(1)}, bf16[8192,128]{1,0:T(8,128)(2,1)}, u32[]{:S(2)}) copy-start(bf16[8192,128]{1,0:T(8,128)(2,1)} %key_weight.1) | copy-start | bytes 6291460
  55.6 3.0 %copy-start.3 = (f32[8192]{0:T(1024)S(1)}, f32[8192]{0:T(1024)}, u32[]{:S(2)}) copy-start(f32[8192]{0:T(1024)} %param.16) | copy-start | bytes 98308
